TPU v7x, 128 devices: a whole 4x4x4 slice. The times are simulated.
128 devices in a mesh: space: 32 (over y, z, x_hi), tm: 4 (over x_lo, core).
Axes of the slice: x: 4 (x_hi: 2, x_lo: 2; x = x_hi * 2 + x_lo), y: 4, z: 4, core: 2. Of those that a mesh axis runs over, the one named last changes fastest.
Arguments:
- pw_field: float32 [96, 128, 36864], P('space', 'tm'), may hold values from -6 to 6
- cell_area: float32 [16, 36864], replicated, may hold values from 0.5 to 1.5
- tile_ids: int32 [96], replicated, may hold values from 0 to 95, as said below
- edge_table: int32 [3, 96, 4], replicated, may hold values from 0 to 95, as said below
Outputs:
- gram: float32 [128, 128], P('tm')
Inputs may be any that keep to these rules, and one draw needn't show every extreme that they name: A permutation: slot s holds the tile of face tile_ids[s] // 16, row (tile_ids[s] // 4) mod 4, column tile_ids[s] mod 4 of the face. `edge_table`: the cube's gluing for the slots of tile_ids: the neighbour slot and edge across each edge, and 1 where the two edges run in opposite directions; flags and edges lie in 0 to 1 and 0 to 3.
All inputs are finite; a program needn't handle non-finite values.
Results may differ from a plain program's by a relative error of at most 0.000051.
Values sent between devices are 32-bit elements; how exact they have to be, the bound alone decides.
No kernel may reach another device: no remote copies, remote signals or barrier semaphores. Data moves between devices by JAX's collectives and lax.ppermute only.
A program may use at most 704 MiB of HBM per device.

v0:
```python
import jax
import jax.numpy as jnp
from jax import lax
from jax.sharding import PartitionSpec as P

STRIDE = 4
STEPS = 4
TILE = 192


def coefficient(step_idx):
    return 0.12 + 0.1 * step_idx / max(STEPS - 1, 1)


def edge_strips(weighted):
    return jnp.stack(
        [
            weighted[:, :, :TILE],
            weighted[:, :, -TILE:],
            weighted[:, :, 0::TILE],
            weighted[:, :, TILE - 1 :: TILE],
        ],
        axis=1,
    )


def pick_halo(all_strips, near_slot, near_edge, near_flip):
    snap_count = all_strips.shape[2]
    edge_width = all_strips.shape[3]
    flat_strips = all_strips.reshape(-1, snap_count, edge_width)
    position = (near_slot * 4 + near_edge).reshape(-1)
    chosen = jnp.take(flat_strips, position, axis=0).reshape(
        near_slot.shape[0], 4, snap_count, edge_width
    )
    return jnp.where((near_flip == 1)[:, :, None, None], chosen[..., ::-1], chosen)


def smooth_step(values, weighted, tile_area, halo_rows, factor):
    column = jnp.arange(TILE * TILE, dtype=jnp.int32) % TILE
    upper_nb = jnp.concatenate([halo_rows[:, 0], weighted[:, :, :-TILE]], axis=2)
    lower_nb = jnp.concatenate([weighted[:, :, TILE:], halo_rows[:, 1]], axis=2)
    left_shift = jnp.concatenate([weighted[:, :, :1], weighted[:, :, :-1]], axis=2)
    right_shift = jnp.concatenate([weighted[:, :, 1:], weighted[:, :, -1:]], axis=2)
    left_nb = jnp.where(column == 0, jnp.repeat(halo_rows[:, 2], TILE, axis=2), left_shift)
    right_nb = jnp.where(column == TILE - 1, jnp.repeat(halo_rows[:, 3], TILE, axis=2), right_shift)
    return (
        values
        + factor * (upper_nb + lower_nb + left_nb + right_nb - 4.0 * weighted) / tile_area[:, None]
    )


def subsample(values):
    shaped = values.reshape(values.shape[0], values.shape[1], TILE, TILE)[
        :, :, 1::STRIDE, 1::STRIDE
    ]
    return shaped.reshape(values.shape[0], values.shape[1], -1)


def body(pw_field, cell_area, tile_ids, edge_table):
    per_dev = pw_field.shape[0]
    snap_count = pw_field.shape[1]
    offset = lax.axis_index("space") * per_dev
    own_ids = lax.dynamic_slice_in_dim(tile_ids, offset, per_dev, 0)
    own_table = lax.dynamic_slice_in_dim(edge_table, offset, per_dev, 1)
    tile_area = jnp.take(cell_area, own_ids % cell_area.shape[0], axis=0)
    values = pw_field
    for step_idx in range(STEPS):
        weighted = tile_area[:, None] * values
        gathered = lax.all_gather(edge_strips(weighted), "space", axis=0, tiled=True)
        halo_rows = pick_halo(gathered, own_table[0], own_table[1], own_table[2])
        values = smooth_step(values, weighted, tile_area, halo_rows, coefficient(step_idx))
    sampled = subsample(values)
    weights = subsample(tile_area[:, None])[:, 0].reshape(-1)
    snap_rows = jnp.transpose(sampled, (1, 0, 2)).reshape(snap_count, -1)
    cell_count = tile_ids.shape[0] * sampled.shape[2]
    weighted_rows = snap_rows * weights
    partial_gram = jnp.dot(
        weighted_rows,
        lax.all_gather(snap_rows, "tm", axis=0, tiled=True).T,
        precision=lax.Precision.HIGHEST,
        preferred_element_type=jnp.float32,
    )
    gram_rows = lax.psum(partial_gram, "space")
    return gram_rows / cell_count


def solution(mesh):
    placed = (P("space", "tm", None), P(), P(), P())
    return jax.shard_map(body, mesh=mesh, in_specs=placed, out_specs=P("tm", None), check_vma=False)
```

profile of v0, /device:TPU:0, one launch (start us, length us, event | category | flops | bytes accessed | tf_op | source)
XLA Modules:
  0.0 1356.2 jit_solution(7140177576354468776)
XLA Ops:
  9.2 11.2 broadcast_multiply_fusion.3
  20.5 7.5 slice.196
  28.0 7.5 slice.195
  35.5 1.0 slice_bitcast_fusion.23
  39.1 18.6 %fusion.45 = (f32[3,32,36672]{2,1,0:T(8,128)}, f32[3,32,36672]{2,1,0:T(8,128)}) fusion(f32[3,32,36864]{2,1,0:T(8,128)} %broadcast_multiply_fusion.3), kind=kLoop, calls=%fused_computation.116 | loop fusion | bytes 56328192 | tf_op jit(solution)/shard_map/slice | solution.py:40
  57.7 18.5 %fusion.47 = (f32[3,32,36863]{2,1,0:T(8,128)}, f32[3,32,36863]{2,1,0:T(8,128)}) fusion(f32[3,32,36864]{2,1,0:T(8,128)} %broadcast_multiply_fusion.3), kind=kLoop, calls=%fused_computation.118 | loop fusion | bytes 56621568 | tf_op jit(solution)/shard_map/slice | solution.py:42
  76.2 94.2 %all-gather.6.cloned.1.call-done = f32[96,4,32,192]{3,2,0,1:T(8,128)} async-done(((f32[3,4,32,192]{3,2,0,1:T(8,128)}), f32[96,4,32,192]{3,2,0,1:T(8,128)}) %all-gather.6.cloned.1.call-update) | async-done | bytes 9437200 | tf_op jit(solution)/shard_map/all_gather | solution.py:69
  170.4 11.9 copy.17
  182.2 5.1 gather_fusion.1
  188.0 7.3 broadcast_in_dim.110
  195.3 18.1 %reshape.114 = f32[3,32,36864]{2,1,0:T(8,128)} reshape(f32[3,32,192,192]{3,2,1,0:T(8,128)} %broadcast_in_dim.110) | data formatting | bytes 28311552 | tf_op jit(solution)/shard_map/reshape | solution.py:45
  213.4 7.3 broadcast_in_dim.108
  220.7 18.2 %reshape.113 = f32[3,32,36864]{2,1,0:T(8,128)} reshape(f32[3,32,192,192]{3,2,1,0:T(8,128)} %broadcast_in_dim.108) | data formatting | bytes 28311552 | tf_op jit(solution)/shard_map/reshape | solution.py:44
  238.9 43.7 %broadcast_multiply_fusion.2 = (f32[3,32,36864]{2,1,0:T(8,128)}, f32[3,32,36864]{2,1,0:T(8,128)}) fusion(f32[3,36864]{1,0:T(4,128)S(1)} %broadcast_select_fusion.1, f32[3,32,36864]{2,1,0:T(8,128)} %param.6, f32[3,32,36864]{2,1,0:T(8,128)} %reshape.114, f32[3,32,1]{2,1,0:T(8,128)S(1)} %get-tuple-element.41, f32[3,32,36863]{2,1,0:T(8,128)} %get-tuple-element.43, ...), kind=kLoop, calls=%fused_computation.43 | loop fusion | flops 56623104 | bytes 127918080 | tf_op jit(solution)/shard_map/mul | solution.py:68
  282.6 7.5 slice.212
  290.1 7.5 slice.211
  297.6 1.0 slice_bitcast_fusion.17
  299.6 1.1 fusion.43
  300.6 21.0 %fusion.42 = (f32[3,32,36672]{2,1,0:T(8,128)}, f32[3,32,36672]{2,1,0:T(8,128)}) fusion(f32[3,32,36864]{2,1,0:T(8,128)} %get-tuple-element.10), kind=kLoop, calls=%fused_computation.113 | loop fusion | bytes 56328192 | tf_op jit(solution)/shard_map/slice | solution.py:40
  321.9 10.6 fusion.44
  332.4 95.6 %all-gather.8.cloned.1.call-done = f32[96,4,32,192]{3,2,0,1:T(8,128)} async-done(((f32[3,4,32,192]{3,2,0,1:T(8,128)}), f32[96,4,32,192]{3,2,0,1:T(8,128)}) %all-gather.8.cloned.1.call-update) | async-done | bytes 9437200 | tf_op jit(solution)/shard_map/all_gather | solution.py:69
  428.0 11.9 copy.18
  439.9 5.1 gather_fusion.2
  445.7 7.3 broadcast_in_dim.112
  453.0 18.1 %reshape.118 = f32[3,32,36864]{2,1,0:T(8,128)} reshape(f32[3,32,192,192]{3,2,1,0:T(8,128)} %broadcast_in_dim.112) | data formatting | bytes 28311552 | tf_op jit(solution)/shard_map/reshape | solution.py:45
  471.1 7.3 broadcast_in_dim.111
  478.4 18.1 %reshape.117 = f32[3,32,36864]{2,1,0:T(8,128)} reshape(f32[3,32,192,192]{3,2,1,0:T(8,128)} %broadcast_in_dim.111) | data formatting | bytes 28311552 | tf_op jit(solution)/shard_map/reshape | solution.py:44
  496.5 43.5 %broadcast_multiply_fusion.1 = (f32[3,32,36864]{2,1,0:T(8,128)}, f32[3,32,36864]{2,1,0:T(8,128)}) fusion(f32[3,36864]{1,0:T(4,128)S(1)} %broadcast_select_fusion.1, f32[3,32,36864]{2,1,0:T(8,128)} %get-tuple-element.11, f32[3,32,36864]{2,1,0:T(8,128)} %reshape.118, f32[3,32,1]{2,1,0:T(8,128)S(1)} %get-tuple-element.33, ...), kind=kLoop, calls=%fused_computation.42 | loop fusion | flops 56623104 | bytes 127918080 | tf_op jit(solution)/shard_map/mul | solution.py:68
  540.0 7.5 slice.226
  547.5 7.5 slice.225
  555.0 1.0 slice_bitcast_fusion.11
  556.9 1.1 fusion.40
  558.0 21.0 %fusion.39 = (f32[3,32,36672]{2,1,0:T(8,128)}, f32[3,32,36672]{2,1,0:T(8,128)}) fusion(f32[3,32,36864]{2,1,0:T(8,128)} %get-tuple-element.8), kind=kLoop, calls=%fused_computation.110 | loop fusion | bytes 56328192 | tf_op jit(solution)/shard_map/slice | solution.py:40
  579.2 10.6 fusion.41
  589.8 95.6 %all-gather.10.cloned.1.call-done = f32[96,4,32,192]{3,2,0,1:T(8,128)} async-done(((f32[3,4,32,192]{3,2,0,1:T(8,128)}), f32[96,4,32,192]{3,2,0,1:T(8,128)}) %all-gather.10.cloned.1.call-update) | async-done | bytes 9437200 | tf_op jit(solution)/shard_map/all_gather | solution.py:69
  685.4 11.9 copy.19
  697.2 5.1 gather_fusion.3
  703.0 7.3 broadcast_in_dim.114
  710.3 18.1 %reshape.122 = f32[3,32,36864]{2,1,0:T(8,128)} reshape(f32[3,32,192,192]{3,2,1,0:T(8,128)} %broadcast_in_dim.114) | data formatting | bytes 28311552 | tf_op jit(solution)/shard_map/reshape | solution.py:45
  728.4 7.3 broadcast_in_dim.113
  735.7 18.2 %reshape.121 = f32[3,32,36864]{2,1,0:T(8,128)} reshape(f32[3,32,192,192]{3,2,1,0:T(8,128)} %broadcast_in_dim.113) | data formatting | bytes 28311552 | tf_op jit(solution)/shard_map/reshape | solution.py:44
  753.9 43.7 %broadcast_multiply_fusion = (f32[3,32,36864]{2,1,0:T(8,128)}, f32[3,32,36864]{2,1,0:T(8,128)}) fusion(f32[3,36864]{1,0:T(4,128)S(1)} %broadcast_select_fusion.1, f32[3,32,36864]{2,1,0:T(8,128)} %get-tuple-element.9, f32[3,32,36864]{2,1,0:T(8,128)} %reshape.122, f32[3,32,1]{2,1,0:T(8,128)S(1)} %get-tuple-element.25, f32[3,32,36863]{2,1,0:T(8,128)} %get-tuple-element.27, ...), kind=kLoop, calls=%fused_computation.41 | loop fusion | flops 56623104 | bytes 127918080 | tf_op jit(solution)/shard_map/mul | solution.py:68
  797.6 7.5 slice.240
  805.1 7.5 slice.239
  812.6 1.0 slice_bitcast_fusion.5
  814.6 1.1 fusion.37
  815.6 21.0 %fusion.38 = (f32[3,32,36672]{2,1,0:T(8,128)}, f32[3,32,36672]{2,1,0:T(8,128)}) fusion(f32[3,32,36864]{2,1,0:T(8,128)} %get-tuple-element.6), kind=kLoop, calls=%fused_computation.109 | loop fusion | bytes 56328192 | tf_op jit(solution)/shard_map/slice | solution.py:41
  836.9 10.6 fusion.36
  847.4 95.6 %all-gather.12.cloned.1.call-done = f32[96,4,32,192]{3,2,0,1:T(8,128)} async-done(((f32[3,4,32,192]{3,2,0,1:T(8,128)}), f32[96,4,32,192]{3,2,0,1:T(8,128)}) %all-gather.12.cloned.1.call-update) | async-done | bytes 9437200 | tf_op jit(solution)/shard_map/all_gather | solution.py:69
  943.0 11.9 copy.20
  954.9 5.1 gather_fusion.4
  960.7 7.3 broadcast_in_dim.116
  968.0 18.1 %reshape.126 = f32[3,32,36864]{2,1,0:T(8,128)} reshape(f32[3,32,192,192]{3,2,1,0:T(8,128)} %broadcast_in_dim.116) | data formatting | bytes 28311552 | tf_op jit(solution)/shard_map/reshape | solution.py:45
  986.1 7.3 broadcast_in_dim.115
  993.4 18.1 %reshape.125 = f32[3,32,36864]{2,1,0:T(8,128)} reshape(f32[3,32,192,192]{3,2,1,0:T(8,128)} %broadcast_in_dim.115) | data formatting | bytes 28311552 | tf_op jit(solution)/shard_map/reshape | solution.py:44
  1011.5 38.3 %fusion.23 = f32[3,32,36864]{2,1,0:T(8,128)} fusion(f32[3,32,36864]{2,1,0:T(8,128)} %get-tuple-element.7, f32[3,32,36672]{2,1,0:T(8,128)} %get-tuple-element.19, f32[3,32,192]{2,1,0:T(8,128)S(1)} %get-tuple-element.49, f32[3,32,192]{2,1,0:T(8,128)S(1)} %get-tuple-element.48, f32[3,32,36672]{2,1,0:T(8,128)} %get-tuple-element.18, ...), kind=kLoop, calls=%fused_computation.38 | loop fusion | flops 53084160 | bytes 113762304 | tf_op jit(solution)/shard_map/add | solution.py:47
  1049.8 18.2 %reshape.127 = f32[3,32,192,192]{3,2,1,0:T(8,128)} reshape(f32[3,32,36864]{2,1,0:T(8,128)} %fusion.23) | data formatting | bytes 28311552 | tf_op jit(solution)/shard_map/reshape | solution.py:53
  1068.1 46.9 %slice.251 = f32[3,32,48,48]{3,2,1,0:T(8,128)} slice(f32[3,32,192,192]{3,2,1,0:T(8,128)} %reshape.127), slice={[0:3:1], [0:32:1], [1:192:4], [1:192:4]} | slice | bytes 1769472 | tf_op jit(solution)/shard_map/slice | solution.py:53
  1115.0 3.1 reshape.128
  1118.1 2.1 copy.22
  1120.8 1.1 slice.252
  1122.0 37.0 %all-gather.14.cloned.1.call-done = f32[128,6912]{1,0:T(8,128)} async-done(((f32[32,6912]{1,0:T(8,128)}), f32[128,6912]{1,0:T(8,128)}) %all-gather.14.cloned.1.call-update) | async-done | bytes 3538960 | tf_op jit(solution)/shard_map/all_gather | solution.py:79
  1159.0 5.8 fusion.24
  1164.8 184.1 %psum.7 = f32[32,128]{1,0:T(8,128)S(1)} all-reduce(f32[32,128]{1,0:T(8,128)S(1)} %fusion.24), channel_id=1, replica_groups=mesh['space'=32,'tm'=4] {'space'}, use_global_device_ids=true, to_apply=%region_0.2 | all-reduce | flops 4096 | bytes 32768 | tf_op jit(solution)/shard_map/psum | solution.py:83
  (89 shorter events, 12.1 us)
Async XLA Ops:
  6.5 1.7 copy-start
  6.5 163.8 %all-gather.6.cloned.1.call-start = ((), (), s32[]{:S(2)}) async-start(), calls=%async_computation | async-start | bytes 12976128 | tf_op jit(solution)/shard_map/all_gather | solution.py:69
  7.4 13.1 copy-start.5
  9.0 11.5 copy-start.2
  9.2 28.4 %copy-start.4 = (s32[3,96,4]{1,2,0:T(4,128)S(1)}, s32[3,96,4]{1,2,0:T(4,128)}, u32[]{:S(2)}) copy-start(s32[3,96,4]{1,2,0:T(4,128)} %param.9) | copy-start | bytes 13828
  37.4 390.7 %all-gather.8.cloned.1.call-start = ((), (), s32[]{:S(2)}) async-start(), calls=%async_computation.1 | async-start | bytes 12976128 | tf_op jit(solution)/shard_map/all_gather | solution.py:69
  299.5 385.9 %all-gather.10.cloned.1.call-start = ((), (), s32[]{:S(2)}) async-start(), calls=%async_computation.2 | async-start | bytes 12976128 | tf_op jit(solution)/shard_map/all_gather | solution.py:69
  299.5 22.1 %slice-start.8 = ((s8[14155776]{0:T(1024)(128)(4,1)}), s8[4194304]{0:T(1024)(128)(4,1)S(1)}, s32[]{:S(2)}) async-start(s8[14155776]{0:T(1024)(128)(4,1)} %bitcast.99), calls=%async_computation.13 | async-start | bytes 8388608
  300.6 21.0 %slice-start.9 = ((s8[14155776]{0:T(1024)(128)(4,1)}), s8[4194304]{0:T(1024)(128)(4,1)S(1)}, s32[]{:S(2)}) async-start(s8[14155776]{0:T(1024)(128)(4,1)} %bitcast.99), calls=%async_computation.14 | async-start | bytes 8388608
  300.6 21.0 %slice-start.10 = ((s8[14155776]{0:T(1024)(128)(4,1)}), s8[4194304]{0:T(1024)(128)(4,1)S(1)}, s32[]{:S(2)}) async-start(s8[14155776]{0:T(1024)(128)(4,1)} %bitcast.99), calls=%async_computation.15 | async-start | bytes 8388608
  300.6 21.2 %slice-start.11 = ((s8[14155776]{0:T(1024)(128)(4,1)}), s8[1572864]{0:T(1024)(128)(4,1)S(1)}, s32[]{:S(2)}) async-start(s8[14155776]{0:T(1024)(128)(4,1)} %bitcast.99), calls=%async_computation.16 | async-start | bytes 3145728
  556.8 386.2 %all-gather.12.cloned.1.call-start = ((), (), s32[]{:S(2)}) async-start(), calls=%async_computation.3 | async-start | bytes 12976128 | tf_op jit(solution)/shard_map/all_gather | solution.py:69
  556.9 22.1 %slice-start = ((s8[14155776]{0:T(1024)(128)(4,1)}), s8[4194304]{0:T(1024)(128)(4,1)S(1)}, s32[]{:S(2)}) async-start(s8[14155776]{0:T(1024)(128)(4,1)} %bitcast.95), calls=%async_computation.5 | async-start | bytes 8388608
  558.0 21.0 %slice-start.1 = ((s8[14155776]{0:T(1024)(128)(4,1)}), s8[4194304]{0:T(1024)(128)(4,1)S(1)}, s32[]{:S(2)}) async-start(s8[14155776]{0:T(1024)(128)(4,1)} %bitcast.95), calls=%async_computation.6 | async-start | bytes 8388608
  558.0 21.0 %slice-start.2 = ((s8[14155776]{0:T(1024)(128)(4,1)}), s8[4194304]{0:T(1024)(128)(4,1)S(1)}, s32[]{:S(2)}) async-start(s8[14155776]{0:T(1024)(128)(4,1)} %bitcast.95), calls=%async_computation.7 | async-start | bytes 8388608
  558.0 21.2 %slice-start.3 = ((s8[14155776]{0:T(1024)(128)(4,1)}), s8[1572864]{0:T(1024)(128)(4,1)S(1)}, s32[]{:S(2)}) async-start(s8[14155776]{0:T(1024)(128)(4,1)} %bitcast.95), calls=%async_computation.8 | async-start | bytes 3145728
  814.5 344.5 %all-gather.14.cloned.1.call-start = ((), (), s32[]{:S(2)}) async-start(), calls=%async_computation.4 | async-start | bytes 4423680 | tf_op jit(solution)/shard_map/all_gather | solution.py:79
  814.5 22.1 %slice-start.4 = ((s8[14155776]{0:T(1024)(128)(4,1)}), s8[4194304]{0:T(1024)(128)(4,1)S(1)}, s32[]{:S(2)}) async-start(s8[14155776]{0:T(1024)(128)(4,1)} %bitcast.97), calls=%async_computation.9 | async-start | bytes 8388608
  815.6 21.0 %slice-start.5 = ((s8[14155776]{0:T(1024)(128)(4,1)}), s8[4194304]{0:T(1024)(128)(4,1)S(1)}, s32[]{:S(2)}) async-start(s8[14155776]{0:T(1024)(128)(4,1)} %bitcast.97), calls=%async_computation.10 | async-start | bytes 8388608
  815.6 21.0 %slice-start.6 = ((s8[14155776]{0:T(1024)(128)(4,1)}), s8[4194304]{0:T(1024)(128)(4,1)S(1)}, s32[]{:S(2)}) async-start(s8[14155776]{0:T(1024)(128)(4,1)} %bitcast.97), calls=%async_computation.11 | async-start | bytes 8388608
  815.6 21.2 %slice-start.7 = ((s8[14155776]{0:T(1024)(128)(4,1)}), s8[1572864]{0:T(1024)(128)(4,1)S(1)}, s32[]{:S(2)}) async-start(s8[14155776]{0:T(1024)(128)(4,1)} %bitcast.97), calls=%async_computation.12 | async-start | bytes 3145728
  1049.8 70.5 %copy-start.3 = (f32[3,36864]{1,0:T(4,128)S(1)}, f32[3,36864]{1,0:T(4,128)}, u32[]{:S(2)}) copy-start(f32[3,36864]{1,0:T(4,128)} %copy-done.2) | copy-start | bytes 1327108
  1049.8 70.8 %copy-start.6 = (pred[3]{0:T(512)(128)(4,1)S(1)}, pred[3]{0:T(512)(128)(4,1)}, u32[]{:S(2)}) copy-start(pred[3]{0:T(512)(128)(4,1)} %copy-done.5) | copy-start | bytes 13
  1049.8 299.7 %copy-start.1 = (f32[16,36864]{1,0:T(8,128)S(1)}, f32[16,36864]{1,0:T(8,128)}, u32[]{:S(2)}) copy-start(f32[16,36864]{1,0:T(8,128)} %param.7) | copy-start | bytes 7077892
Sparse Core Ops, SparseCore 0:
  37.5 132.8 all-gather.5
  299.6 128.3 all-gather.7
  557.0 128.3 all-gather.9
  814.6 128.3 all-gather.11
  1120.4 38.5 all-gather.13
where the time goes:
time: 1360 us
  local copies, waits for them, and re-layouts  547 us (40%)
  waiting for transfers between devices  418 us (31%)
  other arithmetic  187 us (14%)
  blocking collectives  184 us (14%)
  between operations  13.8 us (1%)
    all_gather x4, waiting for transfers between devices, body(): lax.all_gather(edge_strips(weighted), 'space', axis=0, tiled=True)  381 us
    psum x1, blocking collectives, body(): gram_rows = lax.psum(partial_gram, 'space')  184 us
    mul x4, other arithmetic, body(): weighted = tile_area[:, None] * values  142 us
    reshape x4, local copies, waits for them, and re-layouts, smooth_step(): jnp.repeat(halo_rows[:, 2], TILE, axis=2)  72.6 us
    reshape x4, local copies, waits for them, and re-layouts, smooth_step(): jnp.repeat(halo_rows[:, 3], TILE, axis=2)  72.4 us
    slice x3, local copies, waits for them, and re-layouts, smooth_step(): weighted[:, :, :-TILE]  60.6 us
    slice x2, local copies, waits for them, and re-layouts, subsample(): values.reshape(values.shape[0], values.shape[1], TILE, TILE)  48 us
    all_gather x4, local copies, waits for them, and re-layouts, body(): lax.all_gather(edge_strips(weighted), 'space', axis=0, tiled=True)  47.5 us
  transfers between devices with their start and end apart: 5, of which 5 were waited for; matrix products, arithmetic and copies ran while one was open for 10% of the time, Pallas kernels for 0%

commit v1 on v0

v1 whole, which is shorter than its diff:
```python
import functools

import jax
import jax.numpy as jnp
import ml_dtypes
import numpy as np
from jax import lax
from jax.experimental import pallas as pl
from jax.experimental.pallas import tpu as pltpu
from jax.sharding import Mesh
from jax.sharding import PartitionSpec as P

STRIDE = 4
STEPS = 4
TILE = 192
CELLS = TILE * TILE
SAMP = TILE // STRIDE
AXES = ("y", "z", "xh", "xl", "c")
PAD = 640
SB = 16
F32 = jnp.float32
BF16 = jnp.bfloat16


def stencil():
    k = np.zeros((9, 9))
    k[4, 4] = 1.0
    for step in range(STEPS):
        c = 0.12 + 0.1 * step / max(STEPS - 1, 1)
        p = np.pad(k, 1)
        lap = p[:-2, 1:-1] + p[2:, 1:-1] + p[1:-1, :-2] + p[1:-1, 2:] - 4 * k
        k = k + c * lap
    return k[4:, 4:]


K = stencil()


def coef(d, m):
    return float(K[d, m]) if d + m <= STEPS else 0.0


CORNER = coef(2, 2) / 2.0
NEAR = {1: 0, 0: 1, 2: 1, 3: 2}
FAR = {1: 4, 0: 3, 2: 3, 3: 9}


def lane_tables():
    lane = np.arange(128) % 4
    near = np.array([[coef(d, NEAR[l]) for l in lane] for d in range(5)])
    far = np.array([[coef(d, FAR[l]) for l in lane] for d in range(2)])
    return np.concatenate([near, far, np.zeros((1, 128))]).astype(np.float32)


def edge_coef(high, flip, depth, pos):
    m = NEAR[(pos % 4) if not flip else ((3 - pos) % 4)]
    return coef(depth + 2 + high, m)


def row_edge_table():
    out = np.zeros((16, 128))
    for high in range(2):
        for flip in range(2):
            for depth in range(3):
                for lane in range(128):
                    out[(2 * high + flip) * 4 + depth, lane] = edge_coef(high, flip, depth, lane)
    return out.astype(np.float32)


def col_lanes():
    where = {}
    for k in range(8):
        for par in range(2):
            for depth in range(3):
                where[((0 if par == 0 else 64) + depth + 6 * k) % 128] = (2 * k + par, 2, depth)
                where[((63 if par == 0 else 127) - depth + 6 * k) % 128] = (2 * k + par, 3, depth)
    return where


def col_edge_table():
    out = np.zeros((8, 128))
    for lane, (row, edge, depth) in col_lanes().items():
        for high in range(2):
            for flip in range(2):
                out[(edge - 2) * 4 + 2 * high + flip, lane] = edge_coef(high, flip, depth, row)
    return out.astype(np.float32)


def place(lanes, pos, j, value=1.0):
    lanes[pos, j] = value


def sum_matrix():
    s = np.zeros((384, SAMP))
    for c in range(TILE):
        for j in range(SAMP):
            d = abs(c - (4 * j + 1))
            if 3 <= d <= 4:
                s[c, j] = 1.0
            if d <= 2:
                s[192 + c, j] = 1.0
    return s


def quad_matrices():
    s = sum_matrix()
    a = np.zeros((4, 384, 256))
    b = np.zeros((4, 384, 256))
    for q in range(4):
        a[q, :, 48 * q : 48 * q + 48] = s
        a[q, :, 192 + q] = s[:, 0]
        a[q, :, 196 + q] = s[:, SAMP - 1]
        b[q, :, 64 + 48 * q : 64 + 48 * q + 48] = s
        b[q, :, q] = s[:, 0]
        b[q, :, 4 + q] = s[:, SAMP - 1]
    both = np.stack([a.reshape(1536, 256), b.reshape(1536, 256)])
    return both.astype(ml_dtypes.bfloat16)


def row_edge_matrix():
    m = np.zeros((256, 128))
    for pos in range(TILE):
        for j in range(SAMP):
            if abs(pos - (4 * j + 1)) <= 2:
                m[pos, j] = 1.0
            if abs((TILE - 1 - pos) - (4 * j + 1)) <= 2:
                m[pos, 64 + j] = 1.0
    for k in range(2):
        m[192 + k, 48 + k] = 1.0
        m[192 + k, 112 + k] = 1.0
    return m.astype(ml_dtypes.bfloat16)


def col_edge_matrix():
    m = np.zeros((12, 128, 256))
    for group in range(12):
        for lane, (row, edge, _) in col_lanes().items():
            pos = 16 * group + row
            for j in range(SAMP):
                if abs(pos - (4 * j + 1)) <= 2:
                    m[group, lane, (edge - 2) * 128 + j] = 1.0
                if abs((TILE - 1 - pos) - (4 * j + 1)) <= 2:
                    m[group, lane, (edge - 2) * 128 + 64 + j] = 1.0
    return m.reshape(1536, 256).astype(ml_dtypes.bfloat16)


def inner_mask():
    m = np.zeros((8, 384))
    for g in range(6):
        for lane in range(384):
            r, j = 8 * g + lane // 48, lane % 48
            m[g, lane] = float(0 < r < SAMP - 1 and 0 < j < SAMP - 1)
    return m.astype(np.float32)


def halves(v):
    hi = v.astype(BF16)
    return hi, (v - hi.astype(F32)).astype(BF16)


def lanes_of(shape):
    return lax.broadcasted_iota(jnp.int32, shape, len(shape) - 1)


def space_index():
    return lax.axis_index("y") * 8 + lax.axis_index("z") * 2 + lax.axis_index("xh")


def swap_ends(v, lane):
    return jnp.where(
        lane == 0,
        pltpu.roll(v, 128 - (SAMP - 1), 1),
        jnp.where(lane == SAMP - 1, pltpu.roll(v, SAMP - 1, 1), v),
    )


def filter_kernel(
    ids, table, x_ref, area_ref, quad_ref, rowm_ref, colm_ref, lane_ref, rowk_ref, colk_ref, mask_ref,
    keep_ref, send_ref, edge_ref,
    wp, lhs, lhs_area, root, packed, lrow, lcol, strip,
):
    tile, half = pl.program_id(0), pl.program_id(1)
    slot = 3 * space_index() + tile
    aid = ids[slot] % 16
    xl = lax.axis_index("xl")
    lane = lanes_of((SB, 128))
    row0 = pl.multiple_of(tile * 32 + half * SB, SB)

    @pl.when((tile == 0) & (half == 0))
    def _():
        wp[:, :PAD] = jnp.zeros((SB, PAD), F32)
        wp[:, PAD + CELLS :] = jnp.zeros((SB, 512), F32)
        strip[:, 96:, :] = jnp.zeros((8, 32, 128), F32)

    area8 = pl.multiple_of((aid // 8) * 8, 8)
    turn = (8 - aid % 8) % 8

    def area_row(off, size):
        return pltpu.roll(area_ref[pl.ds(area8, 8), pl.ds(off, size)], turn, 0)[0:1]

    def variant(edge):
        at = slot * 4 + edge
        return (table[1, at] & 1) * 2 + table[2, at]

    k2 = colk_ref[pl.ds(variant(2), 1), :] + colk_ref[pl.ds(4 + variant(3), 1), :]

    def weigh(g, _):
        start = pl.multiple_of(g * 3072, 128)
        acc = None
        for k in range(8):
            vs = []
            for part in range(3):
                off = pl.multiple_of(start + (3 * k + part) * 128, 128)
                w = x_ref[0, :, pl.ds(off, 128)] * area_row(off, 128)
                wp[:, pl.ds(pl.multiple_of(off + PAD, 128), 128)] = w
                vs.append(w)
            both = jnp.where(lane < 3, vs[0], jnp.where(lane >= 125, vs[2], vs[1]))
            if k == 0:
                acc = both
            else:
                moved = pltpu.roll(both, 6 * k, 1)
                mine = ((lane >= 6 * k - 3) & (lane < 6 * k + 3)) | ((lane >= 61 + 6 * k) & (lane < 67 + 6 * k))
                acc = jnp.where(mine, moved, acc)
        hi, lo = halves(acc * k2)
        at = pl.multiple_of(g * 128, 128)
        lcol[pl.ds(row0, SB), pl.ds(at, 128)] = hi
        lcol[pl.ds(pl.multiple_of(96 + row0, SB), SB), pl.ds(at, 128)] = lo
        return 0

    lax.fori_loop(0, 12, weigh, 0)

    near = [lane_ref[d : d + 1, :] for d in range(5)]
    far = [lane_ref[5 + d : 6 + d, :] for d in range(2)]
    wide = lambda k: jnp.concatenate([k, k], axis=1)
    near = [wide(k) for k in near]
    far = [wide(k) for k in far]

    def rows(g, _):
        for h in range(8):
            base = pl.multiple_of(g * 6144 + 768 * h + PAD, 128)

            def win(off):
                return wp[:, pl.ds(pl.multiple_of(base + off, 128), 256)]

            s0 = win(128)
            s1 = win(384) + win(0)
            s2 = win(512) + win(-256)
            s3 = win(768) + win(-384)
            s4 = win(896) + win(-640)
            va = near[0] * s0 + near[2] * s2 + near[4] * s4
            vb = near[1] * s1 + near[3] * s3
            v1 = va + pltpu.roll(vb, 64, 1)
            v2 = far[1] * s1 + pltpu.roll(far[0] * s0, 192, 1)
            parts = [v2[:, :128], jnp.where(lane < 64, v2[:, 128:], v1[:, :128]), v1[:, 128:]]
            for p, v in enumerate(parts):
                hi, lo = halves(v)
                at = (h % 4) * 384 + p * 128
                lhs[h // 4, pl.ds(pl.multiple_of(g * SB, SB), SB), at : at + 128] = hi
                lhs[h // 4, pl.ds(pl.multiple_of(96 + g * SB, SB), SB), at : at + 128] = lo
        return 0

    lax.fori_loop(0, 6, rows, 0)

    @pl.when(half == 0)
    def _():
        lane2 = lanes_of((1, 256))
        picked = (lane2 >= 64) & (lane2 % 4 == 1)
        for r in range(SAMP):
            g, h = r // 8, r % 8
            a = area_row(768 * r + 128, 256)
            lhs_area[h // 4, g : g + 1, (h % 4) * 384 : (h % 4) * 384 + 128] = jnp.zeros((1, 128), F32)
            lhs_area[h // 4, g : g + 1, (h % 4) * 384 + 128 : (h % 4) * 384 + 384] = jnp.where(picked, a, 0.0)
        outs = []
        for n in range(2):
            lhs_area[n, 6:16, :] = jnp.zeros((10, 1536), F32)
            v = lhs_area[n]
            hi = v.astype(BF16)
            rest = v - hi.astype(F32)
            mid = rest.astype(BF16)
            low = (rest - mid.astype(F32)).astype(BF16)
            o = jnp.dot(jnp.concatenate([hi, mid, low], axis=0), quad_ref[n], preferred_element_type=F32)
            outs.append(o[0:8] + o[16:24] + o[32:40])
        a, b = outs
        lane8 = lanes_of((8, 128))
        area = jnp.concatenate([a[:, :128], jnp.where(lane8 < 64, a[:, 128:], b[:, :128]), b[:, 128:]], axis=1)
        inner = mask_ref[...] > 0.0
        root[...] = jnp.where(inner, lax.rsqrt(jnp.where(inner, area, 1.0)), 0.0)

    out_a = jnp.dot(lhs[0], quad_ref[0], preferred_element_type=F32)
    out_b = jnp.dot(lhs[1], quad_ref[1], preferred_element_type=F32)
    out_a = out_a[:96] + out_a[96:]
    out_b = out_b[:96] + out_b[96:]
    left = jnp.zeros((SB, 128), F32)
    right = jnp.zeros((SB, 128), F32)
    for g in range(6):
        a, b = out_a[SB * g : SB * g + SB], out_b[SB * g : SB * g + SB]
        a1, b0 = a[:, 128:], b[:, :128]
        packed[g, :, 0:128] = a[:, :128] * root[g : g + 1, 0:128]
        packed[g, :, 128:256] = jnp.where(lane < 64, a1, b0) * root[g : g + 1, 128:256]
        packed[g, :, 256:384] = b[:, 128:] * root[g : g + 1, 256:384]
        at_a = (lane >= 8 * g) & (lane < 8 * g + 4)
        at_b = (lane >= 8 * g + 4) & (lane < 8 * g + 8)
        left = jnp.where(at_a, pltpu.roll(a1, (8 * g + 64) % 128, 1), left)
        left = jnp.where(at_b, pltpu.roll(b0, (8 * g + 4) % 128, 1), left)
        right = jnp.where(at_a, pltpu.roll(a1, (8 * g + 60) % 128, 1), right)
        right = jnp.where(at_b, b0 if g == 0 else pltpu.roll(b0, 8 * g, 1), right)
    keep_ref[...] = packed[pl.ds(3 * xl, 3)]
    send_ref[...] = packed[pl.ds(3 * (1 - xl), 3)]
    here = pl.ds(row0, SB)
    strip[4, here, :] = out_a[:SB, :128]
    strip[5, here, :] = swap_ends(pltpu.roll(out_b[80:96, 128:], 48, 1), lane)
    strip[6, here, :] = left
    strip[7, here, :] = swap_ends(right, lane)

    lane2 = lanes_of((SB, 256))

    def win(off):
        return wp[:, PAD + off : PAD + off + 256]

    for edge in range(2):
        if edge == 0:
            lines = [win(0), pltpu.roll(win(128), 192, 1), win(384)]
        else:
            lines = [pltpu.roll(win(36608), 192, 1), win(36480), pltpu.roll(win(36224), 192, 1)]
        v = variant(edge) * 4
        u = jnp.zeros((SB, 256), F32)
        for d in range(3):
            u = u + wide(rowk_ref[pl.ds(v + d, 1), :]) * lines[d]
        u0 = u[:, :128]
        first, second = lines[0][:, :128], lines[0][:, 128:]
        u1 = jnp.where(
            lane == 64,
            pltpu.roll(first, 64, 1) * CORNER,
            jnp.where(lane == 65, pltpu.roll(second, 2, 1) * CORNER, u[:, 128:]),
        )
        for p, v in enumerate((u0, u1)):
            hi, lo = halves(v)
            lrow[pl.ds(pl.multiple_of(edge * 96 + row0, SB), SB), 128 * p : 128 * p + 128] = hi
            lrow[pl.ds(pl.multiple_of(192 + edge * 96 + row0, SB), SB), 128 * p : 128 * p + 128] = lo

    @pl.when((tile == 2) & (half == 1))
    def _():
        cr = jnp.dot(lrow[...], rowm_ref[...], preferred_element_type=F32)
        cc = jnp.dot(lcol[...], colm_ref[...], preferred_element_type=F32)
        cr = cr[:192] + cr[192:]
        cc = cc[:96] + cc[96:]
        given = [cr[:96], cr[96:], cc[:, :128], cc[:, 128:]]
        lane32 = lanes_of((32, 128))
        for edge in range(4):
            for t in range(3):
                at = (3 * space_index() + t) * 4 + edge
                v = given[edge][32 * t : 32 * t + 32]
                v = jnp.where(table[2, at] == 1, pltpu.roll(v, 64, 1), v)
                strip[edge, 32 * t : 32 * t + 32, :] = jnp.where(table[1, at] & 1 == 1, swap_ends(v, lane32), v)
        turned = []
        for q in range(8):
            tr = jnp.transpose(strip[q])
            edge_ref[pl.ds(q, SAMP, stride=16), :] = tr[:SAMP]
            edge_ref[pl.ds(8 + q, SAMP, stride=16), :] = tr[:SAMP]
            if q < 2:
                turned.append([tr[48:49], tr[49:50]])
        lane1 = lanes_of((1, 128))
        for c in range(2):
            edge_ref[8 * c + 6 : 8 * c + 7, :] = turned[0][0]
            edge_ref[8 * c + 7 : 8 * c + 8, :] = turned[0][1]
            for end in range(2):
                for t in range(3):
                    at = 8 * c + 3 * end + t
                    moved = pltpu.roll(turned[1][end], 96 - 32 * t, 1)
                    edge_ref[at : at + 1, :] = jnp.where(lane1 >= 96, moved, edge_ref[at : at + 1, :])


def gram_kernel(
    ids, table, got_ref, keep_ref, recv_ref, keep2_ref, recv2_ref, area_ref, out_ref,
    z, h, w, areas, hl, full,
):
    xl, c = lax.axis_index("xl"), lax.axis_index("c")
    chip = space_index() * 2 + xl
    first, last = chip == 0, chip == SAMP - 1
    lane = lanes_of((8, 128))
    sub = lax.broadcasted_iota(jnp.int32, (8, 128), 0)

    for ref, row in (
        (keep_ref, 2 * xl + c),
        (recv_ref, 2 * (1 - xl) + c),
        (keep2_ref, 2 * xl + 1 - c),
        (recv2_ref, 2 * (1 - xl) + 1 - c),
    ):
        at = pl.multiple_of(row * 32, 32)
        for b in range(9):
            hi, lo = halves(ref[b])
            hl[pl.ds(at, 32), 384 * b : 384 * b + 384] = hi
            hl[pl.ds(pl.multiple_of(128 + at, 32), 32), 384 * b : 384 * b + 384] = lo

    @pl.when(chip >= SAMP)
    def _():
        hl[:, 3456:] = jnp.zeros((256, 384), BF16)

    @pl.when(chip < SAMP)
    def _():
        def spread(s, _):
            v = [got_ref[pl.ds(pl.multiple_of(s * 32 + 8 * t, 8), 8), :] for t in range(4)]
            for i in range(4):
                acc = v[i]
                for t in range(4):
                    if t != i:
                        acc = jnp.where(lane // 32 == t, pltpu.roll(v[t], (32 * (t - i)) % 128, 1), acc)
                if i < 3:
                    z[pl.ds(pl.multiple_of(s * 24 + 8 * i, 8), 8), :] = acc
                else:
                    z[pl.ds(pl.multiple_of(768 + s * 8, 8), 8), :] = acc
            return 0

        lax.fori_loop(0, 32, spread, 0, unroll=2)

        cell = 4 * chip + 1
        swap = jnp.where(first, 4 * (SAMP - 1) + 1, jnp.where(last, 1, cell))
        spots = (192 + cell, 189 * 192 + swap, cell * 192 + 1, cell * 192 + 189)
        lane16 = lanes_of((16, 128))
        for e, spot in enumerate(spots):
            a = area_ref[:, pl.ds(pl.multiple_of((spot // 128) * 128, 128), 128)]
            a = jnp.sum(jnp.where(lane16 == spot % 128, a, 0.0), axis=1, keepdims=True)
            v = jnp.broadcast_to(lax.rsqrt(a), (16, 128))
            if e >= 2:
                v = jnp.where(first | last, 0.0, v)
            areas[pl.ds(4 + e, 16, stride=8), :] = v

        @pl.when(first)
        def _():
            def corner(slot, _):
                total = z[pl.ds(slot * 8 + 4, 1), :]
                for edge in (0, 2):
                    at = slot * 4 + edge
                    n1, e1, f1 = table[0, at], table[1, at], table[2, at]
                    side = n1 * 4 + 2 * (1 - (e1 >> 1)) + f1
                    n2, e2, f2 = table[0, side], table[1, side], table[2, side]
                    b2 = (e1 & 1) ^ f2
                    row = jnp.where(e2 < 2, e2, b2)
                    col = jnp.where(e2 < 2, b2, e2 - 2)
                    s2 = n2 // 3
                    spare = 768 + s2 * 8 + 3 * col + (n2 - 3 * s2)
                    where = jnp.where(row == 0, n2 * 8 + 6 + col, spare)
                    total = total + z[pl.ds(where, 1), :]
                h[pl.ds(slot, 1), :] = total
                return 0

            lax.fori_loop(0, 96, corner, 0)

            def put(slot, _):
                z[pl.ds(slot * 8 + 4, 1), :] = h[pl.ds(slot, 1), :]
                return 0

            lax.fori_loop(0, 96, put, 0)

        def gather(slot, _):
            for e in range(4):
                at = slot * 4 + e
                h[pl.ds(slot * 8 + 4 + e, 1), :] = z[pl.ds(table[0, at] * 8 + table[1, at], 1), :]
            return 0

        lax.fori_loop(0, 96, gather, 0, unroll=4)
        fx = jnp.where(first, 1.0, 0.0)
        fy = jnp.where(last, 1.0, 0.0)

        def total(pair, _):
            both = []
            for n in range(2):
                slot = pair * 2 + n
                at = pl.ds(pl.multiple_of(slot * 8, 8), 8)
                hv = jnp.where(sub >= 4, h[at, :], 0.0)
                extra = fx * pltpu.roll(hv, 6, 0) + fy * jnp.where(sub == 4, pltpu.roll(hv, 5, 0), pltpu.roll(hv, 7, 0))
                v = z[at, :] + hv + jnp.where(sub < 6, extra, 0.0)
                both.append(v * areas[pl.ds(pl.multiple_of((ids[slot] % 16) * 8, 8), 8), :])
            w[pl.ds(pl.multiple_of(pair * 8, 8), 8), :] = jnp.where(sub < 4, pltpu.roll(both[0], 4, 0), both[1])
            return 0

        lax.fori_loop(0, 48, total, 0, unroll=2)
        for p in range(3):
            hi, lo = halves(jnp.transpose(w[128 * p : 128 * p + 128, :]))
            at = 3456 + 128 * p
            hl[:128, at : at + 128] = hi
            hl[128:, at : at + 128] = lo

    g = lax.dot_general(hl[:128], hl[...], (((1,), (1,)), ((), ())), preferred_element_type=F32)
    cross = g[:, 128:]
    full[...] = g[:, :128] + cross + jnp.transpose(cross)
    for k in range(2):
        block = full[pl.ds(pl.multiple_of(64 * k + 32 * c, 32), 32), :]
        out_ref[k] = block
        out_ref[2 + k] = block


def body(pw_field, cell_area, tile_ids, edge_table):
    table = edge_table.reshape(3, 384)
    consts = [
        quad_matrices(), row_edge_matrix(), col_edge_matrix(), lane_tables(), row_edge_table(), col_edge_table(), inner_mask(),
    ]
    consts = [jnp.asarray(v) for v in consts]
    whole = lambda v: pl.BlockSpec(v.shape, functools.partial(lambda n, *_: (0,) * n, v.ndim), pipeline_mode=pl.Buffered(1))
    part = pl.BlockSpec((3, SB, 384), lambda i, h, *_: (i, h, 0))
    keep, send, edges = pl.pallas_call(
        filter_kernel,
        grid_spec=pltpu.PrefetchScalarGridSpec(
            num_scalar_prefetch=2,
            grid=(3, 2),
            in_specs=[pl.BlockSpec((1, SB, CELLS), lambda i, h, *_: (i, h, 0)), whole(cell_area)] + [whole(v) for v in consts],
            out_specs=[part, part, pl.BlockSpec((1024, 128), lambda i, h, *_: (0, 0))],
            scratch_shapes=[
                pltpu.VMEM((SB, PAD + CELLS + 512), F32),
                pltpu.VMEM((2, 192, 1536), BF16),
                pltpu.VMEM((2, 16, 1536), F32),
                pltpu.VMEM((8, 384), F32),
                pltpu.VMEM((6, SB, 384), F32),
                pltpu.VMEM((384, 256), BF16),
                pltpu.VMEM((192, 1536), BF16),
                pltpu.VMEM((8, 128, 128), F32),
            ],
        ),
        out_shape=[
            jax.ShapeDtypeStruct((9, 32, 384), F32),
            jax.ShapeDtypeStruct((9, 32, 384), F32),
            jax.ShapeDtypeStruct((1024, 128), F32),
        ],
        compiler_params=pltpu.CompilerParams(dimension_semantics=("arbitrary", "arbitrary"), vmem_limit_bytes=48 * 2**20),
        name="filter",
    )(tile_ids, table, pw_field, cell_area, *consts)

    flip = [(0, 1), (1, 0)]
    recv = lax.ppermute(send, "xl", flip)
    keep2 = lax.ppermute(keep, "c", flip)
    got = lax.all_to_all(edges.reshape(128, 8, 128), AXES, 0, 0).reshape(1024, 128)
    recv2 = lax.ppermute(recv, "c", flip)
    vm = pl.BlockSpec(memory_space=pltpu.VMEM)
    sm = pl.BlockSpec(memory_space=pltpu.SMEM)
    rows = pl.pallas_call(
        gram_kernel,
        in_specs=[sm, sm] + [vm] * 6,
        out_specs=vm,
        scratch_shapes=[
            pltpu.VMEM((1024, 128), F32),
            pltpu.VMEM((768, 128), F32),
            pltpu.VMEM((384, 128), F32),
            pltpu.VMEM((128, 128), F32),
            pltpu.VMEM((256, 3840), BF16),
            pltpu.VMEM((128, 128), F32),
        ],
        out_shape=jax.ShapeDtypeStruct((4, 32, 128), F32),
        compiler_params=pltpu.CompilerParams(vmem_limit_bytes=48 * 2**20),
        name="gram",
    )(tile_ids, table, got, keep, recv, keep2, recv2, cell_area)
    line = jnp.sum(lax.all_to_all(rows, ("xh", "xl"), 0, 0), axis=0)
    spread = jnp.broadcast_to(line[None], (16, 32, 128))
    return jnp.sum(lax.all_to_all(spread, ("y", "z"), 0, 0), axis=0) / (96 * SAMP * SAMP)


def solution(mesh):
    fine = Mesh(mesh.devices.reshape(4, 4, 2, 2, 2), AXES)
    tm = ("xl", "c")
    placed = (P(("y", "z", "xh"), tm, None), P(), P(), P())
    return jax.shard_map(body, mesh=fine, in_specs=placed, out_specs=P(tm, None), check_vma=False)
```

time: 1360 us -> 91.2 us (0.07)
  local copies, waits for them, and re-layouts: 547 us -> 9.57 us
  waiting for transfers between devices: 418 us -> 12.2 us
  other arithmetic: 187 us -> 0.64 us
  blocking collectives: 184 us -> 19.1 us
  Pallas kernels: 0 us -> 36.1 us
  between operations: 13.8 us -> 0.09 us
    all_gather x5 -> x0, waiting for transfers between devices: 418 us -> none  [the longest x4 381 us: body(): lax.all_gather(edge_strips(weighted), 'space', axis=0, tiled=True)]
    slice x22 -> x0, local copies, waits for them, and re-layouts: 244 us -> none  [the longest x3 60.6 us: smooth_step(): weighted[:, :, :-TILE]]
    psum x1 -> x0, blocking collectives: 184 us -> none  [body(): gram_rows = lax.psum(partial_gram, 'space')]
    reshape x11 -> x1, local copies, waits for them, and re-layouts: 169 us -> 0.14 us  [body(): table = edge_table.reshape(3, 384)]
    mul x4 -> x0, other arithmetic: 142 us -> none  [body(): weighted = tile_area[:, None] * values]
    broadcast_in_dim x8 -> x1, local copies, waits for them, and re-layouts: 58.3 us -> 0.02 us  [body(): spread = jnp.broadcast_to(line[None], (16, 32, 128))]
    all_gather x4 -> x0, local copies, waits for them, and re-layouts: 47.5 us -> none  [body(): lax.all_gather(edge_strips(weighted), 'space', axis=0, tiled=True)]
    add x2 -> x0, other arithmetic: 38.4 us -> none  [the longest x1 38.3 us: smooth_step(): values + factor * (upper_nb + lower_nb + left_nb + right_nb - 4.0 * weigh...]
  transfers between devices with their start and end apart: 5 -> 4, of which waited for: 5 -> 2; matrix products, arithmetic and copies ran while one was open for 10% -> 0% of each run, Pallas kernels for 0% -> 0%
where the time goes in v1:
time: 91.2 us; the launch traced here: 90.6 us
  Pallas kernels  36.1 us (40%)
  blocking collectives  19.1 us (21%)
  starting transfers between devices  12.9 us (14%)
  waiting for transfers between devices  12.2 us (13%)
  local copies, waits for them, and re-layouts  9.57 us (10%)
    pallas_call x1, Pallas kernels, body(): pl.pallas_call(filter_kernel, grid_spec=pltpu.PrefetchScalarGridSpec(num_...  25.8 us
    all_to_all x1, blocking collectives, body(): lax.all_to_all(spread, ('y', 'z'), 0, 0)  11.1 us
    all_to_all x1, waiting for transfers between devices, body(): lax.all_to_all(edges.reshape(128, 8, 128), AXES, 0, 0).reshape(1024, 128)  10.9 us
    all_to_all x1, starting transfers between devices, body(): lax.all_to_all(edges.reshape(128, 8, 128), AXES, 0, 0).reshape(1024, 128)  10.8 us
    pallas_call x1, Pallas kernels, body(): pl.pallas_call(gram_kernel, in_specs=[sm, sm] + [vm] * 6, out_specs=vm, s...  10.3 us
    unnamed x25, local copies, waits for them, and re-layouts  9.4 us
    all_to_all x1, blocking collectives, body(): line = jnp.sum(lax.all_to_all(rows, ('xh', 'xl'), 0, 0), axis=0)  7.99 us
  transfers between devices with their start and end apart: 4, of which 2 were waited for; matrix products, arithmetic and copies ran while one was open for 0% of the time, Pallas kernels for 0%

profile of v1, /device:TPU:0, one launch (start us, length us, event | category | flops | bytes accessed | tf_op | source)
XLA Modules:
  0.0 90.6 jit_solution(5443705522674175824)
XLA Ops:
  0.0 0.8 copy.14
  0.8 0.1 reshape.10.table
  1.0 0.0 copy-start.1
  1.0 1.4 %copy-done.1 = bf16[2,1536,256]{2,1,0:T(8,128)(2,1)S(1)} copy-done((bf16[2,1536,256]{2,1,0:T(8,128)(2,1)S(1)}, bf16[2,1536,256]{2,1,0:T(8,128)(2,1)}, u32[]{:S(2)}) %copy-start.1) | copy-done | bytes 1572888
  2.4 0.0 copy-start.2
  2.4 1.1 %copy-done.2 = bf16[1536,256]{1,0:T(8,128)(2,1)S(1)} copy-done((bf16[1536,256]{1,0:T(8,128)(2,1)S(1)}, bf16[1536,256]{1,0:T(8,128)(2,1)}, u32[]{:S(2)}) %copy-start.2) | copy-done | bytes 786456
  3.5 0.0 copy-start.5
  3.5 0.8 copy-done.5
  4.3 0.0 copy-start.6
  4.3 0.7 copy-done.6
  5.1 0.0 copy-start.7
  5.1 0.7 copy-done.7
  5.7 0.0 copy-start.8
  5.8 0.7 copy-done.8
  6.4 0.0 copy-start.9
  6.4 0.7 copy-done.9
  7.1 0.0 copy-start.10
  7.1 0.7 copy-done.10
  7.8 0.0 copy-start
  7.8 0.0 copy-start.11
  7.8 25.8 %filter.1 = (f32[9,32,384]{2,1,0:T(8,128)S(1)}, f32[9,32,384]{2,1,0:T(8,128)}, f32[1024,128]{1,0:T(8,128)}) custom-call(s32[96]{0:T(128)S(1)} %copy-done.10, s32[3,384]{1,0:T(4,128)S(1)} %reshape.10.table, f32[3,32,36864]{2,1,0:T(8,128)} %x_ref.1, f32[16,36864]{1,0:T(8,128)} %area_ref.3, bf16[2,1536,256]{2,1,0:T(8,128)(2,1)S(1)} %copy-done.1, ...), custom_call_target="tpu_custom_call" | custom-call | tf_op jit(solution)/shard_map/filter/pallas_call | solution.py:501
  33.6 1.6 %collective-permute-start = (f32[9,32,384]{2,1,0:T(8,128)}, f32[9,32,384]{2,1,0:T(8,128)}, u32[]{:S(2)}, u32[]{:S(2)}) collective-permute-start(f32[9,32,384]{2,1,0:T(8,128)} %get-tuple-element.10), channel_id=1, source_target_pairs={{0,2},{2,0},{1,3},{3,1},{4,6},{6,4},{5,7},{7,5},{8,10},{10,8},{9,1... | collective-permute-start | bytes 1327112 | tf_op jit(solution)/shard_map/ppermute | solution.py:529
  35.1 10.8 %all-to-all-start = ((f32[128,8,128]{2,1,0:T(8,128)}), f32[128,8,128]{2,1,0:T(8,128)S(1)}, u32[]{:S(2)}, u32[]{:S(2)}) async-start(f32[128,8,128]{2,1,0:T(8,128)} %bitcast), calls=%async_computation | async-start | bytes 1048576 | tf_op jit(solution)/shard_map/all_to_all | solution.py:531
  45.9 0.1 collective-permute-start.1
  46.0 0.0 collective-permute-done.recv_ref
  46.0 0.5 collective-permute-start.2
  46.5 1.3 %collective-permute-done.1.keep2_ref = f32[9,32,384]{2,1,0:T(8,128)S(1)} collective-permute-done((f32[9,32,384]{2,1,0:T(8,128)S(1)}, f32[9,32,384]{2,1,0:T(8,128)S(1)}, u32[]{:S(2)}, u32[]{:S(2)}) %collective-permute-start.1) | collective-permute-done | bytes 442400 | tf_op jit(solution)/shard_map/ppermute | solution.py:530
  47.8 0.0 copy-start.3
  47.8 0.8 copy-done.3
  48.6 10.9 %all-to-all-done = f32[128,8,128]{2,1,0:T(8,128)S(1)} async-done(((f32[128,8,128]{2,1,0:T(8,128)}), f32[128,8,128]{2,1,0:T(8,128)S(1)}, u32[]{:S(2)}, u32[]{:S(2)}) %all-to-all-start) | async-done | bytes 524320 | tf_op jit(solution)/shard_map/all_to_all | solution.py:531
  59.5 0.0 collective-permute-done.2.recv2_ref
  59.5 0.0 copy-done
  59.5 0.0 copy-done.11
  59.5 0.0 copy-start.4
  59.5 1.0 %copy-done.4 = f32[9,32,384]{2,1,0:T(8,128)S(1)} copy-done((f32[9,32,384]{2,1,0:T(8,128)S(1)}, f32[9,32,384]{2,1,0:T(8,128)}, u32[]{:S(2)}) %copy-start.4) | copy-done | bytes 442392
  60.5 10.3 %gram.1 = f32[4,32,128]{2,1,0:T(8,128)S(1)} custom-call(s32[96]{0:T(128)S(1)} %copy-done.11, s32[3,384]{1,0:T(4,128)S(1)} %reshape.10.table, f32[1024,128]{1,0:T(8,128)S(1)} %bitcast.2, f32[9,32,384]{2,1,0:T(8,128)S(1)} %get-tuple-element.9.keep_ref, f32[9,32,384]{2,1,0:T(8,128)} %collective-permute-done.recv_ref, f32[9,32,384]{2,1,0:T(8,128)S(1)} %copy-done.4, ...), custom_call_target="tpu_custom_call" | custom-call | tf_op jit(solution)/shard_map/gram/pallas_call | solution.py:535
  70.9 8.0 %all_to_all.15 = f32[4,32,128]{2,1,0:T(8,128)S(1)} all-to-all(f32[4,32,128]{2,1,0:T(8,128)S(1)} %gram.1), channel_id=1, replica_groups=mesh['y'=4,'z'=4,'xh'=2,'xl'=2,'c'=2] {'xh','xl'}, dimensions={0} | all-to-all | bytes 131072 | tf_op jit(solution)/shard_map/all_to_all | solution.py:551
  78.9 11.1 %all_to_all.16 = f32[16,32,128]{2,1,0:T(8,128)S(1)} all-to-all(f32[16,32,128]{2,1,0:T(8,128)S(1)} %broadcast_in_dim.2), channel_id=1, replica_groups=mesh['y'=4,'z'=4,'xh'=2,'xl'=2,'c'=2] {'y','z'}, dimensions={0} | all-to-all | bytes 524288 | tf_op jit(solution)/shard_map/all_to_all | solution.py:553
  90.0 0.6 broadcast_multiply_fusion
  (3 shorter events, 0.0 us)
Async XLA Ops:
  1.0 1.4 %copy-start.1 = (bf16[2,1536,256]{2,1,0:T(8,128)(2,1)S(1)}, bf16[2,1536,256]{2,1,0:T(8,128)(2,1)}, u32[]{:S(2)}) copy-start(bf16[2,1536,256]{2,1,0:T(8,128)(2,1)} %constant.19.clone.quad_ref) | copy-start | bytes 4718596
  2.4 1.1 %copy-start.2 = (bf16[1536,256]{1,0:T(8,128)(2,1)S(1)}, bf16[1536,256]{1,0:T(8,128)(2,1)}, u32[]{:S(2)}) copy-start(bf16[1536,256]{1,0:T(8,128)(2,1)} %constant.21.clone.colm_ref) | copy-start | bytes 2359300
  3.5 0.8 copy-start.5
  4.3 0.7 copy-start.6
  5.1 0.7 copy-start.7
  5.7 0.7 copy-start.8
  6.4 0.7 copy-start.9
  7.1 0.7 copy-start.10
  7.8 51.7 %copy-start = (f32[16,36864]{1,0:T(8,128)S(1)}, f32[16,36864]{1,0:T(8,128)}, u32[]{:S(2)}) copy-start(f32[16,36864]{1,0:T(8,128)} %area_ref.3) | copy-start | bytes 7077892
  7.8 51.7 %copy-start.11 = (s32[96]{0:T(128)S(1)}, s32[96]{0:T(128)}, u32[]{:S(2)}) copy-start(s32[96]{0:T(128)} %ids.3) | copy-start | bytes 1156
  33.6 12.5 %collective-permute-start = (f32[9,32,384]{2,1,0:T(8,128)}, f32[9,32,384]{2,1,0:T(8,128)}, u32[]{:S(2)}, u32[]{:S(2)}) collective-permute-start(f32[9,32,384]{2,1,0:T(8,128)} %get-tuple-element.10), channel_id=1, source_target_pairs={{0,2},{2,0},{1,3},{3,1},{4,6},{6,4},{5,7},{7,5},{8,10},{10,8},{9,1... | collective-permute-start | bytes 1327112 | tf_op jit(solution)/shard_map/ppermute | solution.py:529
  35.1 24.4 %all-to-all-start = ((f32[128,8,128]{2,1,0:T(8,128)}), f32[128,8,128]{2,1,0:T(8,128)S(1)}, u32[]{:S(2)}, u32[]{:S(2)}) async-start(f32[128,8,128]{2,1,0:T(8,128)} %bitcast), calls=%async_computation | async-start | bytes 1048576 | tf_op jit(solution)/shard_map/all_to_all | solution.py:531
  45.9 1.9 %collective-permute-start.1 = (f32[9,32,384]{2,1,0:T(8,128)S(1)}, f32[9,32,384]{2,1,0:T(8,128)S(1)}, u32[]{:S(2)}, u32[]{:S(2)}) collective-permute-start(f32[9,32,384]{2,1,0:T(8,128)S(1)} %get-tuple-element.9.keep_ref), channel_id=1, source_target_pairs={{0,1},{1,0},{2,3},{3,2},{4,5},{5,4},{6,7},{7,6},{8,9},{9,8},{10,11... | collective-permute-start | bytes 1327112 | tf_op jit(solution)/shard_map/ppermute | solution.py:530
  46.0 13.5 %collective-permute-start.2 = (f32[9,32,384]{2,1,0:T(8,128)}, f32[9,32,384]{2,1,0:T(8,128)}, u32[]{:S(2)}, u32[]{:S(2)}) collective-permute-start(f32[9,32,384]{2,1,0:T(8,128)} %collective-permute-done.recv_ref), channel_id=1, source_target_pairs={{0,1},{1,0},{2,3},{3,2},{4,5},{5,4},{6,7},{7,6},{8,9},{9,8},{10,11... | collective-permute-start | bytes 1327112 | tf_op jit(solution)/shard_map/ppermute | solution.py:532
  47.8 0.8 copy-start.3
  59.5 1.0 %copy-start.4 = (f32[9,32,384]{2,1,0:T(8,128)S(1)}, f32[9,32,384]{2,1,0:T(8,128)}, u32[]{:S(2)}) copy-start(f32[9,32,384]{2,1,0:T(8,128)} %copy-done.3) | copy-start | bytes 1327108

commit v2 on v0

v2 whole, which is shorter than its diff:
```python
import functools

import jax
import jax.numpy as jnp
import ml_dtypes
import numpy as np
from jax import lax
from jax.experimental import pallas as pl
from jax.experimental.pallas import tpu as pltpu
from jax.sharding import Mesh
from jax.sharding import PartitionSpec as P

STRIDE = 4
STEPS = 4
TILE = 192
CELLS = TILE * TILE
SAMP = TILE // STRIDE
AXES = ("y", "z", "xh", "xl", "c")
PAD = 640
SB = 32
PARTS = 4
PART = CELLS // PARTS
VMEM_LIMIT = 60 * 2**20
F32 = jnp.float32
BF16 = jnp.bfloat16


def stencil():
    k = np.zeros((9, 9))
    k[4, 4] = 1.0
    for step in range(STEPS):
        c = 0.12 + 0.1 * step / max(STEPS - 1, 1)
        p = np.pad(k, 1)
        lap = p[:-2, 1:-1] + p[2:, 1:-1] + p[1:-1, :-2] + p[1:-1, 2:] - 4 * k
        k = k + c * lap
    return k[4:, 4:]


K = stencil()


def coef(d, m):
    return float(K[d, m]) if d + m <= STEPS else 0.0


CORNER = coef(2, 2) / 2.0
NEAR = {1: 0, 0: 1, 2: 1, 3: 2}
FAR = {1: 4, 0: 3, 2: 3, 3: 9}


def lane_tables():
    lane = np.arange(128) % 4
    near = np.array([[coef(d, NEAR[l]) for l in lane] for d in range(5)])
    far = np.array([[coef(d, FAR[l]) for l in lane] for d in range(2)])
    return np.concatenate([near, far, np.zeros((1, 128))]).astype(np.float32)


def edge_coef(high, flip, depth, pos):
    m = NEAR[(pos % 4) if not flip else ((3 - pos) % 4)]
    return coef(depth + 2 + high, m)


def row_edge_table():
    out = np.zeros((16, 128))
    for high in range(2):
        for flip in range(2):
            for depth in range(3):
                for lane in range(128):
                    out[(2 * high + flip) * 4 + depth, lane] = edge_coef(high, flip, depth, lane)
    return out.astype(np.float32)


def col_lanes():
    where = {}
    for k in range(8):
        for par in range(2):
            for depth in range(3):
                where[((0 if par == 0 else 64) + depth + 6 * k) % 128] = (2 * k + par, 2, depth)
                where[((63 if par == 0 else 127) - depth + 6 * k) % 128] = (2 * k + par, 3, depth)
    return where


def col_edge_table():
    out = np.zeros((8, 128))
    for lane, (row, edge, depth) in col_lanes().items():
        for high in range(2):
            for flip in range(2):
                out[(edge - 2) * 4 + 2 * high + flip, lane] = edge_coef(high, flip, depth, row)
    return out.astype(np.float32)


def place(lanes, pos, j, value=1.0):
    lanes[pos, j] = value


def sum_matrix():
    s = np.zeros((384, SAMP))
    for c in range(TILE):
        for j in range(SAMP):
            d = abs(c - (4 * j + 1))
            if 3 <= d <= 4:
                s[c, j] = 1.0
            if d <= 2:
                s[192 + c, j] = 1.0
    return s


def quad_matrices():
    s = sum_matrix()
    a = np.zeros((4, 384, 256))
    b = np.zeros((4, 384, 256))
    for q in range(4):
        a[q, :, 48 * q : 48 * q + 48] = s
        a[q, :, 192 + q] = s[:, 0]
        a[q, :, 196 + q] = s[:, SAMP - 1]
        b[q, :, 64 + 48 * q : 64 + 48 * q + 48] = s
        b[q, :, q] = s[:, 0]
        b[q, :, 4 + q] = s[:, SAMP - 1]
    both = np.stack([a.reshape(1536, 256), b.reshape(1536, 256)])
    return both.astype(ml_dtypes.bfloat16)


def row_edge_matrix():
    m = np.zeros((256, 128))
    for pos in range(TILE):
        for j in range(SAMP):
            if abs(pos - (4 * j + 1)) <= 2:
                m[pos, j] = 1.0
            if abs((TILE - 1 - pos) - (4 * j + 1)) <= 2:
                m[pos, 64 + j] = 1.0
    for k in range(2):
        m[192 + k, 48 + k] = 1.0
        m[192 + k, 112 + k] = 1.0
    return m.astype(ml_dtypes.bfloat16)


def col_edge_matrix():
    m = np.zeros((12, 128, 256))
    for group in range(12):
        for lane, (row, edge, _) in col_lanes().items():
            pos = 16 * group + row
            for j in range(SAMP):
                if abs(pos - (4 * j + 1)) <= 2:
                    m[group, lane, (edge - 2) * 128 + j] = 1.0
                if abs((TILE - 1 - pos) - (4 * j + 1)) <= 2:
                    m[group, lane, (edge - 2) * 128 + 64 + j] = 1.0
    return m.reshape(1536, 256).astype(ml_dtypes.bfloat16)


def inner_mask():
    m = np.zeros((8, 384))
    for g in range(6):
        for lane in range(384):
            r, j = 8 * g + lane // 48, lane % 48
            m[g, lane] = float(0 < r < SAMP - 1 and 0 < j < SAMP - 1)
    return m.astype(np.float32)


def halves(v):
    hi = v.astype(BF16)
    return hi, (v - hi.astype(F32)).astype(BF16)


def lanes_of(shape):
    return lax.broadcasted_iota(jnp.int32, shape, len(shape) - 1)


def space_index():
    return lax.axis_index("y") * 8 + lax.axis_index("z") * 2 + lax.axis_index("xh")


def swap_ends(v, lane):
    return jnp.where(
        lane == 0,
        pltpu.roll(v, 128 - (SAMP - 1), 1),
        jnp.where(lane == SAMP - 1, pltpu.roll(v, SAMP - 1, 1), v),
    )


def filter_kernel(
    ids, table, x_hbm, area_hbm, quad_hbm, colm_hbm, rowm_ref, small_ref, mask_ref,
    keep_ref, send_ref, edge_ref, areas_ref,
    xs, area, quads, colm, wp, lhs, stage, root, packed, lrow, lcol, strip, sem_x, sem_a, sem_c,
):
    xl = lax.axis_index("xl")
    lane = lanes_of((SB, 128))
    first_slot = 3 * space_index()

    def copy_x(tile, part):
        at = pl.ds(part * PART, PART)
        return pltpu.make_async_copy(x_hbm.at[tile, :, at], xs.at[tile, :, at], sem_x.at[tile * PARTS + part])

    def copy_area(part):
        at = pl.ds(part * PART, PART)
        return pltpu.make_async_copy(area_hbm.at[:, at], area.at[:, at], sem_a.at[part])

    copy_quads = pltpu.make_async_copy(quad_hbm, quads, sem_c.at[0])
    copy_colm = pltpu.make_async_copy(colm_hbm, colm, sem_c.at[1])
    for part in range(2):
        copy_area(part).start()
        copy_x(0, part).start()
    wp[:, :PAD] = jnp.zeros((SB, PAD), F32)
    wp[:, PAD + CELLS :] = jnp.zeros((SB, 512), F32)
    strip[:, 96:, :] = jnp.zeros((8, 32, 128), F32)
    stage[...] = jnp.zeros((2, 2, 16, 1536), F32)
    wide = lambda k: jnp.concatenate([k, k], axis=1)
    near = [wide(small_ref[d : d + 1, :]) for d in range(5)]
    far = [wide(small_ref[5 + d : 6 + d, :]) for d in range(2)]
    lane2 = lanes_of((SB, 256))
    lane_one = lanes_of((1, 256))
    picked = (lane_one >= 64) & (lane_one % 4 == 1)

    def win(off):
        return wp[:, PAD + off : PAD + off + 256]

    def collect(tile):
        if tile == 0:
            copy_quads.wait()
        outs, area_outs = [], []
        for n in range(2):
            v = stage[tile % 2, n]
            hi = v.astype(BF16)
            rest = v - hi.astype(F32)
            mid = rest.astype(BF16)
            lhs[tile % 2, n, 384:400, :] = hi
            lhs[tile % 2, n, 400:416, :] = mid
            lhs[tile % 2, n, 416:432, :] = (rest - mid.astype(F32)).astype(BF16)
            o = jnp.dot(lhs[tile % 2, n], quads[n], preferred_element_type=F32)
            outs.append(o[:192] + o[192:384])
            area_outs.append(o[384:392] + o[400:408] + o[416:424])
        out_a, out_b = outs
        a, b = area_outs
        lane8 = lanes_of((8, 128))
        mean = jnp.concatenate([a[:, :128], jnp.where(lane8 < 64, a[:, 128:], b[:, :128]), b[:, 128:]], axis=1)
        inner = mask_ref[...] > 0.0
        root[...] = jnp.where(inner, lax.rsqrt(jnp.where(inner, mean, 1.0)), 0.0)

        left = jnp.zeros((SB, 128), F32)
        right = jnp.zeros((SB, 128), F32)
        for g in range(6):
            a, b = out_a[SB * g : SB * g + SB], out_b[SB * g : SB * g + SB]
            a1, b0 = a[:, 128:], b[:, :128]
            packed[g, :, 0:128] = a[:, :128] * root[g : g + 1, 0:128]
            packed[g, :, 128:256] = jnp.where(lane < 64, a1, b0) * root[g : g + 1, 128:256]
            packed[g, :, 256:384] = b[:, 128:] * root[g : g + 1, 256:384]
            at_a = (lane >= 8 * g) & (lane < 8 * g + 4)
            at_b = (lane >= 8 * g + 4) & (lane < 8 * g + 8)
            left = jnp.where(at_a, pltpu.roll(a1, (8 * g + 64) % 128, 1), left)
            left = jnp.where(at_b, pltpu.roll(b0, (8 * g + 4) % 128, 1), left)
            right = jnp.where(at_a, pltpu.roll(a1, (8 * g + 60) % 128, 1), right)
            right = jnp.where(at_b, b0 if g == 0 else pltpu.roll(b0, 8 * g, 1), right)
        keep_ref[3 * tile : 3 * tile + 3] = packed[pl.ds(3 * xl, 3)]
        send_ref[3 * tile : 3 * tile + 3] = packed[pl.ds(3 * (1 - xl), 3)]
        here = slice(32 * tile, 32 * tile + 32)
        strip[4, here, :] = out_a[:SB, :128]
        strip[5, here, :] = swap_ends(pltpu.roll(out_b[160:192, 128:], 48, 1), lane)
        strip[6, here, :] = left
        strip[7, here, :] = swap_ends(right, lane)


    for tile in range(3):
        slot = first_slot + tile
        aid = ids[slot] % 16
        area8 = pl.multiple_of((aid // 8) * 8, 8)
        turn = (8 - aid % 8) % 8
        row0 = tile * 32

        def area_row(off, size):
            return pltpu.roll(area[pl.ds(area8, 8), off : off + size], turn, 0)[0:1]

        def variant(edge):
            return (table[1, edge, slot] & 1) * 2 + table[2, edge, slot]

        k2 = small_ref[pl.ds(24 + variant(2), 1), :] + small_ref[pl.ds(28 + variant(3), 1), :]

        for q in range(PARTS):
            if tile == 0:
                copy_area(q).wait()
            copy_x(tile, q).wait()
            if tile == 0 and q + 2 < PARTS:
                copy_area(q + 2).start()
                copy_x(0, q + 2).start()
            if q == 1 and tile == 0:
                copy_quads.start()
            if q == 1 and tile < 2:
                for n in range(PARTS):
                    copy_x(tile + 1, n).start()
            if q == 1 and tile == 1:
                copy_colm.start()
            for g in range(3 * q, 3 * q + 3):
                acc = None
                for k in range(8):
                    vs = []
                    for part in range(3):
                        off = g * 3072 + (3 * k + part) * 128
                        w = xs[tile, :, off : off + 128] * area_row(off, 128)
                        wp[:, PAD + off : PAD + off + 128] = w
                        vs.append(w)
                    both = jnp.where(lane < 3, vs[0], jnp.where(lane >= 125, vs[2], vs[1]))
                    if k == 0:
                        acc = both
                    else:
                        moved = pltpu.roll(both, 6 * k, 1)
                        mine = ((lane >= 6 * k - 3) & (lane < 6 * k + 3)) | ((lane >= 61 + 6 * k) & (lane < 67 + 6 * k))
                        acc = jnp.where(mine, moved, acc)
                hi, lo = halves(acc * k2)
                lcol[row0 : row0 + SB, g * 128 : g * 128 + 128] = hi
                lcol[96 + row0 : 96 + row0 + SB, g * 128 : g * 128 + 128] = lo

            if q == 1 and tile > 0:
                collect(tile - 1)
            for r in range(max(0, 12 * q - 1), 12 * q + 11 if q < PARTS - 1 else SAMP):
                g, h = r // 8, r % 8
                base = 768 * r
                s0 = win(base + 128)
                s1 = win(base + 384) + win(base)
                s2 = win(base + 512) + win(base - 256)
                s3 = win(base + 768) + win(base - 384)
                s4 = win(base + 896) + win(base - 640)
                va = near[0] * s0 + near[2] * s2 + near[4] * s4
                vb = near[1] * s1 + near[3] * s3
                v1 = va + pltpu.roll(vb, 64, 1)
                v2 = far[1] * s1 + pltpu.roll(far[0] * s0, 192, 1)
                parts = [v2[:, :128], jnp.where(lane < 64, v2[:, 128:], v1[:, :128]), v1[:, 128:]]
                for p, v in enumerate(parts):
                    hi, lo = halves(v)
                    at = (h % 4) * 384 + p * 128
                    lhs[tile % 2, h // 4, g * SB : g * SB + SB, at : at + 128] = hi
                    lhs[tile % 2, h // 4, 192 + g * SB : 192 + g * SB + SB, at : at + 128] = lo
                at = (h % 4) * 384 + 128
                stage[tile % 2, h // 4, g : g + 1, at : at + 256] = jnp.where(picked, area_row(base + 128, 256), 0.0)

        for edge in range(2):
            if edge == 0:
                lines = [win(0), pltpu.roll(win(128), 192, 1), win(384)]
            else:
                lines = [pltpu.roll(win(36608), 192, 1), win(36480), pltpu.roll(win(36224), 192, 1)]
            v = variant(edge) * 4
            u = jnp.zeros((SB, 256), F32)
            for d in range(3):
                u = u + wide(small_ref[pl.ds(8 + v + d, 1), :]) * lines[d]
            first, second = lines[0][:, :128], lines[0][:, 128:]
            u1 = jnp.where(
                lane == 64,
                pltpu.roll(first, 64, 1) * CORNER,
                jnp.where(lane == 65, pltpu.roll(second, 2, 1) * CORNER, u[:, 128:]),
            )
            for p, v in enumerate((u[:, :128], u1)):
                hi, lo = halves(v)
                at = edge * 96 + row0
                lrow[at : at + SB, 128 * p : 128 * p + 128] = hi
                lrow[192 + at : 192 + at + SB, 128 * p : 128 * p + 128] = lo

    collect(2)
    copy_colm.wait()
    cr = jnp.dot(lrow[...], rowm_ref[...], preferred_element_type=F32)
    cc = jnp.dot(lcol[...], colm[...], preferred_element_type=F32)
    cr = cr[:192] + cr[192:]
    cc = cc[:96] + cc[96:]
    given = [cr[:96], cr[96:], cc[:, :128], cc[:, 128:]]
    for edge in range(4):
        for t in range(3):
            slot = first_slot + t
            v = given[edge][32 * t : 32 * t + 32]
            v = jnp.where(table[2, edge, slot] == 1, pltpu.roll(v, 64, 1), v)
            strip[edge, 32 * t : 32 * t + 32, :] = jnp.where(table[1, edge, slot] & 1 == 1, swap_ends(v, lane), v)
    turned = []
    for q in range(8):
        tr = jnp.transpose(strip[q])
        edge_ref[pl.ds(q, SAMP, stride=8), :] = tr[:SAMP]
        if q < 2:
            turned.append([tr[48:49], tr[49:50]])
    lane1 = lanes_of((1, 128))
    edge_ref[6:7, :] = turned[0][0]
    edge_ref[7:8, :] = turned[0][1]
    for end in range(2):
        for t in range(3):
            at = 3 * end + t
            moved = pltpu.roll(turned[1][end], 96 - 32 * t, 1)
            edge_ref[at : at + 1, :] = jnp.where(lane1 >= 96, moved, edge_ref[at : at + 1, :])

    chip = space_index() * 2 + xl
    ends = (chip == 0) | (chip == SAMP - 1)
    place = jnp.minimum(chip, SAMP - 1)
    cell = 4 * place + 1
    swap = 4 * jnp.where(ends, SAMP - 1 - place, place) + 1
    lane16 = lanes_of((16, 128))
    for e, spot in enumerate((192 + cell, 189 * 192 + swap, cell * 192 + 1, cell * 192 + 189)):
        a = area[:, pl.ds(pl.multiple_of((spot // 128) * 128, 128), 128)]
        a = jnp.sum(jnp.where(lane16 == spot % 128, a, 0.0), axis=1, keepdims=True)
        v = jnp.broadcast_to(lax.rsqrt(a), (16, 128))
        if e >= 2:
            v = jnp.where(ends, 0.0, v)
        areas_ref[16 * e : 16 * e + 16, :] = v


def inner_kernel(keep_ref, recv_ref, keep2_ref, recv2_ref, out_ref, hl):
    xl, c = lax.axis_index("xl"), lax.axis_index("c")
    for ref, row in (
        (keep_ref, 2 * xl + c),
        (recv_ref, 2 * (1 - xl) + c),
        (keep2_ref, 2 * xl + 1 - c),
        (recv2_ref, 2 * (1 - xl) + 1 - c),
    ):
        at = pl.multiple_of(row * 32, 32)
        for b in range(9):
            hi, lo = halves(ref[b])
            hl[pl.ds(at, 32), 384 * b : 384 * b + 384] = hi
            hl[pl.ds(pl.multiple_of(128 + at, 32), 32), 384 * b : 384 * b + 384] = lo
    out_ref[...] = self_product(hl[...])


def self_product(hl):
    g = lax.dot_general(hl[:128], hl, (((1,), (1,)), ((), ())), preferred_element_type=F32)
    cross = g[:, 128:]
    return g[:, :128] + cross + jnp.transpose(cross)


def edge_kernel(ids_ref, table_ref, got_ref, got2_ref, areas, inner_ref, out_ref, z, near, sel, full):
    xl, c = lax.axis_index("xl"), lax.axis_index("c")
    chip = space_index() * 2 + xl
    first, last = chip == 0, chip == SAMP - 1
    lane = lanes_of((8, 128))
    full[...] = inner_ref[...]

    @pl.when(chip < SAMP)
    def _():
        even = c == 0
        for s in range(32):
            v = []
            for x in range(2):
                at = s * 16 + 8 * x
                mine, other = got_ref[at : at + 8, :], got2_ref[at : at + 8, :]
                v += [jnp.where(even, mine, other), jnp.where(even, other, mine)]
            for i in range(4):
                acc = v[i]
                for t in range(4):
                    if t != i:
                        acc = jnp.where(lane // 32 == t, pltpu.roll(v[t], (32 * (t - i)) % 128, 1), acc)
                at = s * 24 + 8 * i if i < 3 else 768 + s * 8
                z[at : at + 8, :] = acc

        near[...] = jnp.full((16, 128), -1, jnp.int32)
        for k in range(3):
            near[4 * k : 4 * k + 4, :96] = table_ref[k]
        near[12:13, :96] = ids_ref[...] % 16
        lane1 = lanes_of((1, 128))
        used = lane1 < 96

        def line(k, e):
            return near[4 * k + e : 4 * k + e + 1, :]

        none = jnp.full((1, 128), -1, jnp.int32)
        pos = [jnp.where(used, line(0, e) * 8 + line(1, e), -1) for e in range(4)]
        own = [jnp.where(used, lane1 * 8 + 4 + e, -1) for e in range(4)]
        near[13:15, :] = jnp.full((2, 128), -1, jnp.int32)

        @pl.when(first)
        def _():
            sub = lax.broadcasted_iota(jnp.int32, (128, 128), 0)
            for n, edge in enumerate((0, 2)):
                n1, e1, f1 = line(0, edge), line(1, edge), line(2, edge)
                side = 2 * (1 - (e1 >> 1)) + f1
                found = jnp.zeros((16, 128), F32)
                for e in range(4):
                    one = jnp.where((sub == n1) & (side == e), 1.0, 0.0).astype(BF16)
                    rows = jnp.concatenate([line(0, e), line(1, e), line(2, e), jnp.zeros((13, 128), jnp.int32)], axis=0)
                    rows = jnp.where(lanes_of((16, 128)) < 96, rows, 0).astype(F32).astype(BF16)
                    found = found + jnp.dot(rows, one, preferred_element_type=F32)
                found = found.astype(jnp.int32)
                n2, e2, f2 = found[0:1], found[1:2], found[2:3]
                b2 = (e1 & 1) ^ f2
                row = jnp.where(e2 < 2, e2, b2)
                col = jnp.where(e2 < 2, b2, e2 - 2)
                s2 = (n2 * 43) >> 7
                spare = 768 + s2 * 8 + 3 * col + (n2 - 3 * s2)
                near[13 + n : 14 + n, :] = jnp.where(used, jnp.where(row == 0, n2 * 8 + 6 + col, spare), -1)

        more0 = jnp.where(first, pos[2], jnp.where(last, pos[3], none))
        more1 = jnp.where(first, pos[3], jnp.where(last, pos[2], none))
        picks = [
            [own[0], pos[0], more0, near[13:14, :], near[14:15, :]],
            [own[1], pos[1], more1],
            [own[2], pos[2]],
            [own[3], pos[3]],
        ]
        sub = lax.broadcasted_iota(jnp.int32, (128, 128), 0)
        for block in range(8):
            at = sub + 128 * block
            for e in range(4):
                total = jnp.zeros((128, 128), F32)
                for p in picks[e]:
                    total = total + jnp.where(at == p, 1.0, 0.0)
                sel[128 * block : 128 * block + 128, 128 * e : 128 * e + 128] = total.astype(BF16)
        sub16 = lax.broadcasted_iota(jnp.int32, (16, 128), 0)
        mine = sub16 == near[12:13, :]
        weight = [jnp.sum(jnp.where(mine, areas[16 * e : 16 * e + 16, :], 0.0), axis=0, keepdims=True) for e in range(4)]
        turned = jnp.concatenate([jnp.transpose(z[128 * b : 128 * b + 128, :]) for b in range(8)], axis=1)
        hi, lo = halves(turned)
        both = jnp.dot(jnp.concatenate([hi, lo], axis=0), sel[...], preferred_element_type=F32)
        hi, lo = halves((both[:128] + both[128:]) * jnp.concatenate(weight, axis=1))
        full[...] += self_product(jnp.concatenate([hi, lo], axis=0))

    for k in range(2):
        block = full[pl.ds(pl.multiple_of(64 * k + 32 * c, 32), 32), :]
        out_ref[k] = block
        out_ref[2 + k] = block


def body(pw_field, cell_area, tile_ids, edge_table):
    table = jnp.transpose(edge_table, (0, 2, 1))
    small = jnp.asarray(np.concatenate([lane_tables(), row_edge_table(), col_edge_table()]))
    vm = pl.BlockSpec(memory_space=pltpu.VMEM)
    sm = pl.BlockSpec(memory_space=pltpu.SMEM)
    hbm = pl.BlockSpec(memory_space=pl.ANY)
    keep, send, edges, areas = pl.pallas_call(
        filter_kernel,
        in_specs=[sm, sm] + [hbm] * 4 + [vm] * 3,
        out_specs=[vm] * 4,
        scratch_shapes=[
            pltpu.VMEM((3, SB, CELLS), F32),
            pltpu.VMEM((16, CELLS), F32),
            pltpu.VMEM((2, 1536, 256), BF16),
            pltpu.VMEM((1536, 256), BF16),
            pltpu.VMEM((SB, PAD + CELLS + 512), F32),
            pltpu.VMEM((2, 2, 432, 1536), BF16),
            pltpu.VMEM((2, 2, 16, 1536), F32),
            pltpu.VMEM((8, 384), F32),
            pltpu.VMEM((6, SB, 384), F32),
            pltpu.VMEM((384, 256), BF16),
            pltpu.VMEM((192, 1536), BF16),
            pltpu.VMEM((8, 128, 128), F32),
            pltpu.SemaphoreType.DMA((3 * PARTS,)),
            pltpu.SemaphoreType.DMA((PARTS,)),
            pltpu.SemaphoreType.DMA((2,)),
        ],
        out_shape=[
            jax.ShapeDtypeStruct((9, 32, 384), F32),
            jax.ShapeDtypeStruct((9, 32, 384), F32),
            jax.ShapeDtypeStruct((512, 128), F32),
            jax.ShapeDtypeStruct((64, 128), F32),
        ],
        compiler_params=pltpu.CompilerParams(vmem_limit_bytes=VMEM_LIMIT),
        name="filter",
    )(
        tile_ids, table, pw_field, cell_area, jnp.asarray(quad_matrices()), jnp.asarray(col_edge_matrix()),
        jnp.asarray(row_edge_matrix()), small, jnp.asarray(inner_mask()),
    )

    flip = [(0, 1), (1, 0)]
    recv = lax.ppermute(send, "xl", flip)
    keep2 = lax.ppermute(keep, "c", flip)
    got = lax.all_to_all(edges.reshape(64, 8, 128), AXES[:4], 0, 0).reshape(512, 128)
    got2 = lax.ppermute(got, "c", flip)
    recv2 = lax.ppermute(recv, "c", flip)
    inner = pl.pallas_call(
        inner_kernel,
        in_specs=[vm] * 4,
        out_specs=vm,
        scratch_shapes=[pltpu.VMEM((256, 3456), BF16)],
        out_shape=jax.ShapeDtypeStruct((128, 128), F32),
        compiler_params=pltpu.CompilerParams(vmem_limit_bytes=VMEM_LIMIT),
        name="inner",
    )(keep, recv, keep2, recv2)
    rows = pl.pallas_call(
        edge_kernel,
        in_specs=[vm] * 6,
        out_specs=vm,
        scratch_shapes=[
            pltpu.VMEM((1024, 128), F32),
            pltpu.VMEM((16, 128), jnp.int32),
            pltpu.VMEM((1024, 512), BF16),
            pltpu.VMEM((128, 128), F32),
        ],
        out_shape=jax.ShapeDtypeStruct((4, 32, 128), F32),
        compiler_params=pltpu.CompilerParams(vmem_limit_bytes=VMEM_LIMIT),
        name="edge",
    )(tile_ids.reshape(1, 96), table, got, got2, areas, inner)
    line = jnp.sum(lax.all_to_all(rows, ("xh", "xl"), 0, 0), axis=0)
    spread = jnp.broadcast_to(line[None], (16, 32, 128))
    return jnp.sum(lax.all_to_all(spread, ("y", "z"), 0, 0), axis=0) / (96 * SAMP * SAMP)


def solution(mesh):
    fine = Mesh(mesh.devices.reshape(4, 4, 2, 2, 2), AXES)
    tm = ("xl", "c")
    placed = (P(("y", "z", "xh"), tm, None), P(), P(), P())
    return jax.shard_map(body, mesh=fine, in_specs=placed, out_specs=P(tm, None), check_vma=False)
```

time: 1360 us -> 67.4 us (0.05)
  local copies, waits for them, and re-layouts: 547 us -> 2.28 us
  waiting for transfers between devices: 418 us -> 10 us
  other arithmetic: 187 us -> 0.64 us
  blocking collectives: 184 us -> 20.3 us
  Pallas kernels: 0 us -> 20.3 us
  between operations: 13.8 us -> 0.09 us
    all_gather x5 -> x0, waiting for transfers between devices: 418 us -> none  [the longest x4 381 us: body(): lax.all_gather(edge_strips(weighted), 'space', axis=0, tiled=True)]
    slice x22 -> x0, local copies, waits for them, and re-layouts: 244 us -> none  [the longest x3 60.6 us: smooth_step(): weighted[:, :, :-TILE]]
    psum x1 -> x0, blocking collectives: 184 us -> none  [body(): gram_rows = lax.psum(partial_gram, 'space')]
    reshape x11 -> x0, local copies, waits for them, and re-layouts: 169 us -> none  [the longest x4 72.6 us: smooth_step(): jnp.repeat(halo_rows[:, 2], TILE, axis=2)]
    mul x4 -> x0, other arithmetic: 142 us -> none  [body(): weighted = tile_area[:, None] * values]
    broadcast_in_dim x8 -> x1, local copies, waits for them, and re-layouts: 58.3 us -> 0.02 us  [body(): spread = jnp.broadcast_to(line[None], (16, 32, 128))]
    all_gather x4 -> x0, local copies, waits for them, and re-layouts: 47.5 us -> none  [body(): lax.all_gather(edge_strips(weighted), 'space', axis=0, tiled=True)]
    add x2 -> x0, other arithmetic: 38.4 us -> none  [the longest x1 38.3 us: smooth_step(): values + factor * (upper_nb + lower_nb + left_nb + right_nb - 4.0 * weigh...]
  transfers between devices with their start and end apart: 5 -> 5, of which waited for: 5 -> 1; matrix products, arithmetic and copies ran while one was open for 10% -> 0% of each run, Pallas kernels for 0% -> 5%
where the time goes in v2:
time: 67.4 us; the launch traced here: 67 us
  Pallas kernels  20.3 us (30%)
  blocking collectives  20.3 us (30%)
  starting transfers between devices  13.3 us (20%)
  waiting for transfers between devices  10 us (15%)
  local copies, waits for them, and re-layouts  2.28 us (3%)
    pallas_call x1, Pallas kernels, body(): pl.pallas_call(filter_kernel, in_specs=[sm, sm] + [hbm] * 4 + [vm] * 3, o...  13.5 us
    all_to_all x1, blocking collectives, body(): lax.all_to_all(spread, ('y', 'z'), 0, 0)  11.4 us
    all_to_all x1, starting transfers between devices, body(): lax.all_to_all(edges.reshape(64, 8, 128), AXES[:4], 0, 0).reshape(512, 128)  11.1 us
    all_to_all x1, waiting for transfers between devices, body(): lax.all_to_all(edges.reshape(64, 8, 128), AXES[:4], 0, 0).reshape(512, 128)  10 us
    all_to_all x1, blocking collectives, body(): line = jnp.sum(lax.all_to_all(rows, ('xh', 'xl'), 0, 0), axis=0)  8.87 us
    pallas_call x1, Pallas kernels, body(): pl.pallas_call(edge_kernel, in_specs=[vm] * 6, out_specs=vm, scratch_shap...  3.76 us
    pallas_call x1, Pallas kernels, body(): pl.pallas_call(inner_kernel, in_specs=[vm] * 4, out_specs=vm, scratch_sha...  3.05 us
    unnamed x10, local copies, waits for them, and re-layouts  2.26 us
  transfers between devices with their start and end apart: 5, of which 1 were waited for; matrix products, arithmetic and copies ran while one was open for 0% of the time, Pallas kernels for 5%

profile of v2, /device:TPU:0, one launch (start us, length us, event | category | flops | bytes accessed | tf_op | source)
XLA Modules:
  0.0 67.0 jit_solution(85066691119616535)
XLA Ops:
  0.0 13.5 %filter.1 = (f32[9,32,384]{2,1,0:T(8,128)}, f32[9,32,384]{2,1,0:T(8,128)}, f32[512,128]{1,0:T(8,128)}, f32[64,128]{1,0:T(8,128)}) custom-call(s32[96]{0:T(128)} %ids.1, s32[3,4,96]{2,1,0:T(4,128)} %bitcast.7, f32[3,32,36864]{2,1,0:T(8,128)} %x_hbm.1, f32[16,36864]{1,0:T(8,128)} %area_hbm.1, bf16[2,1536,256]{2,1,0:T(8,128)(2,1)} %constant.16.clone.quad_hbm, ...), custom_call_target="tpu_custom_call" | custom-call | tf_op jit(solution)/shard_map/filter/pallas_call | solution.py:516
  13.5 1.7 %collective-permute-start.1 = (f32[9,32,384]{2,1,0:T(8,128)}, f32[9,32,384]{2,1,0:T(8,128)S(1)}, u32[]{:S(2)}, u32[]{:S(2)}) collective-permute-start(f32[9,32,384]{2,1,0:T(8,128)} %get-tuple-element.12), channel_id=1, source_target_pairs={{0,2},{2,0},{1,3},{3,1},{4,6},{6,4},{5,7},{7,5},{8,10},{10,8},{9,1... | collective-permute-start | bytes 1327112 | tf_op jit(solution)/shard_map/ppermute | solution.py:551
  15.1 11.1 %all-to-all-start = ((f32[64,8,128]{2,1,0:T(8,128)}), f32[64,8,128]{2,1,0:T(8,128)S(1)}, u32[]{:S(2)}, u32[]{:S(2)}) async-start(f32[64,8,128]{2,1,0:T(8,128)} %bitcast.6), calls=%async_computation | async-start | bytes 524288 | tf_op jit(solution)/shard_map/all_to_all | solution.py:553
  26.3 0.1 collective-permute-start.2
  26.4 0.0 collective-permute-done.1.recv_ref
  26.4 0.0 copy-start.1
  26.4 0.5 collective-permute-start.3
  26.9 10.0 %all-to-all-done = f32[64,8,128]{2,1,0:T(8,128)S(1)} async-done(((f32[64,8,128]{2,1,0:T(8,128)}), f32[64,8,128]{2,1,0:T(8,128)S(1)}, u32[]{:S(2)}, u32[]{:S(2)}) %all-to-all-start) | async-done | bytes 262176 | tf_op jit(solution)/shard_map/all_to_all | solution.py:553
  36.9 0.0 copy-start
  36.9 0.0 collective-permute-start
  36.9 0.0 collective-permute-done.2.keep2_ref
  36.9 0.0 copy-start.2
  36.9 0.0 collective-permute-done.3.recv2_ref
  36.9 0.0 copy-done.1
  36.9 0.8 %copy-done.2 = f32[9,32,384]{2,1,0:T(8,128)} copy-done((f32[9,32,384]{2,1,0:T(8,128)}, f32[9,32,384]{2,1,0:T(8,128)S(1)}, u32[]{:S(2)}) %copy-start.2) | copy-done | bytes 442392
  37.7 0.0 copy-start.3
  37.7 0.8 %copy-done.3 = f32[9,32,384]{2,1,0:T(8,128)} copy-done((f32[9,32,384]{2,1,0:T(8,128)}, f32[9,32,384]{2,1,0:T(8,128)S(1)}, u32[]{:S(2)}) %copy-start.3) | copy-done | bytes 442392
  38.5 3.1 %inner.1.inner_ref = f32[128,128]{1,0:T(8,128)} custom-call(f32[9,32,384]{2,1,0:T(8,128)} %get-tuple-element.11.keep_ref, f32[9,32,384]{2,1,0:T(8,128)} %copy-done.1, f32[9,32,384]{2,1,0:T(8,128)} %copy-done.2, f32[9,32,384]{2,1,0:T(8,128)} %copy-done.3), custom_call_target="tpu_custom_call" | custom-call | tf_op jit(solution)/shard_map/inner/pallas_call | solution.py:556
  41.5 0.0 collective-permute-done.got2_ref
  41.5 0.0 copy-start.4
  41.5 0.0 copy-done
  41.5 0.7 %copy-done.4 = f32[512,128]{1,0:T(8,128)} copy-done((f32[512,128]{1,0:T(8,128)}, f32[512,128]{1,0:T(8,128)S(1)}, u32[]{:S(2)}) %copy-start.4) | copy-done | bytes 262168
  42.2 3.8 %edge.1 = f32[4,32,128]{2,1,0:T(8,128)} custom-call(s32[1,96]{1,0:T(1,128)} %bitcast.9, s32[3,4,96]{2,1,0:T(4,128)} %bitcast.8, f32[512,128]{1,0:T(8,128)} %bitcast.5, f32[512,128]{1,0:T(8,128)} %copy-done.4, f32[64,128]{1,0:T(8,128)} %get-tuple-element.10.areas, f32[128,128]{1,0:T(8,128)} %inner.1.inner_ref), custom_call_target="tpu_custom_call" | custom-call | tf_op jit(solution)/shard_map/edge/pallas_call | solution.py:565
  46.0 8.9 %all_to_all.15 = f32[4,32,128]{2,1,0:T(8,128)S(1)} all-to-all(f32[4,32,128]{2,1,0:T(8,128)} %edge.1), channel_id=1, replica_groups=mesh['y'=4,'z'=4,'xh'=2,'xl'=2,'c'=2] {'xh','xl'}, dimensions={0} | all-to-all | bytes 131072 | tf_op jit(solution)/shard_map/all_to_all | solution.py:579
  54.9 11.4 %all_to_all.16 = f32[16,32,128]{2,1,0:T(8,128)S(1)} all-to-all(f32[16,32,128]{2,1,0:T(8,128)S(1)} %broadcast_in_dim.2), channel_id=1, replica_groups=mesh['y'=4,'z'=4,'xh'=2,'xl'=2,'c'=2] {'y','z'}, dimensions={0} | all-to-all | bytes 524288 | tf_op jit(solution)/shard_map/all_to_all | solution.py:581
  66.4 0.6 broadcast_multiply_fusion
  (3 shorter events, 0.0 us)
Async XLA Ops:
  13.5 12.9 %collective-permute-start.1 = (f32[9,32,384]{2,1,0:T(8,128)}, f32[9,32,384]{2,1,0:T(8,128)S(1)}, u32[]{:S(2)}, u32[]{:S(2)}) collective-permute-start(f32[9,32,384]{2,1,0:T(8,128)} %get-tuple-element.12), channel_id=1, source_target_pairs={{0,2},{2,0},{1,3},{3,1},{4,6},{6,4},{5,7},{7,5},{8,10},{10,8},{9,1... | collective-permute-start | bytes 1327112 | tf_op jit(solution)/shard_map/ppermute | solution.py:551
  15.1 21.7 %all-to-all-start = ((f32[64,8,128]{2,1,0:T(8,128)}), f32[64,8,128]{2,1,0:T(8,128)S(1)}, u32[]{:S(2)}, u32[]{:S(2)}) async-start(f32[64,8,128]{2,1,0:T(8,128)} %bitcast.6), calls=%async_computation | async-start | bytes 524288 | tf_op jit(solution)/shard_map/all_to_all | solution.py:553
  26.3 10.6 %collective-permute-start.2 = (f32[9,32,384]{2,1,0:T(8,128)}, f32[9,32,384]{2,1,0:T(8,128)S(1)}, u32[]{:S(2)}, u32[]{:S(2)}) collective-permute-start(f32[9,32,384]{2,1,0:T(8,128)} %get-tuple-element.11.keep_ref), channel_id=1, source_target_pairs={{0,1},{1,0},{2,3},{3,2},{4,5},{5,4},{6,7},{7,6},{8,9},{9,8},{10,11... | collective-permute-start | bytes 1327112 | tf_op jit(solution)/shard_map/ppermute | solution.py:552
  26.4 10.5 %copy-start.1 = (f32[9,32,384]{2,1,0:T(8,128)}, f32[9,32,384]{2,1,0:T(8,128)S(1)}, u32[]{:S(2)}) copy-start(f32[9,32,384]{2,1,0:T(8,128)S(1)} %collective-permute-done.1.recv_ref) | copy-start | bytes 1327108
  26.4 10.5 %collective-permute-start.3 = (f32[9,32,384]{2,1,0:T(8,128)S(1)}, f32[9,32,384]{2,1,0:T(8,128)S(1)}, u32[]{:S(2)}, u32[]{:S(2)}) collective-permute-start(f32[9,32,384]{2,1,0:T(8,128)S(1)} %collective-permute-done.1.recv_ref), channel_id=1, source_target_pairs={{0,1},{1,0},{2,3},{3,2},{4,5},{5,4},{6,7},{7,6},{8,9},{9,8},{10,11... | collective-permute-start | bytes 1327112 | tf_op jit(solution)/shard_map/ppermute | solution.py:555
  36.9 4.7 %copy-start = (f32[64,8,128]{2,1,0:T(8,128)}, f32[64,8,128]{2,1,0:T(8,128)S(1)}, u32[]{:S(2)}) copy-start(f32[64,8,128]{2,1,0:T(8,128)S(1)} %all-to-all-done) | copy-start | bytes 786436
  36.9 4.7 %collective-permute-start = (f32[512,128]{1,0:T(8,128)S(1)}, f32[512,128]{1,0:T(8,128)S(1)}, u32[]{:S(2)}, u32[]{:S(2)}) collective-permute-start(f32[512,128]{1,0:T(8,128)S(1)} %bitcast.4), channel_id=1, source_target_pairs={{0,1},{1,0},{2,3},{3,2},{4,5},{5,4},{6,7},{7,6},{8,9},{9,8},{10,11... | collective-permute-start | bytes 786440 | tf_op jit(solution)/shard_map/ppermute | solution.py:554
  36.9 0.8 %copy-start.2 = (f32[9,32,384]{2,1,0:T(8,128)}, f32[9,32,384]{2,1,0:T(8,128)S(1)}, u32[]{:S(2)}) copy-start(f32[9,32,384]{2,1,0:T(8,128)S(1)} %collective-permute-done.2.keep2_ref) | copy-start | bytes 1327108
  37.7 0.8 %copy-start.3 = (f32[9,32,384]{2,1,0:T(8,128)}, f32[9,32,384]{2,1,0:T(8,128)S(1)}, u32[]{:S(2)}) copy-start(f32[9,32,384]{2,1,0:T(8,128)S(1)} %collective-permute-done.3.recv2_ref) | copy-start | bytes 1327108
  41.5 0.7 %copy-start.4 = (f32[512,128]{1,0:T(8,128)}, f32[512,128]{1,0:T(8,128)S(1)}, u32[]{:S(2)}) copy-start(f32[512,128]{1,0:T(8,128)S(1)} %collective-permute-done.got2_ref) | copy-start | bytes 786436

commit v3 on v2

--- a/solution.py
+++ b/solution.py
@@ -394,17 +394,19 @@
         areas_ref[16 * e : 16 * e + 16, :] = v
 
 
-def inner_kernel(keep_ref, recv_ref, keep2_ref, recv2_ref, out_ref, hl):
+def inner_kernel(keep_ref, recv_ref, keep2_ref, recv2_ref, out_ref, buf, hl, sem):
     xl, c = lax.axis_index("xl"), lax.axis_index("c")
-    for ref, row in (
-        (keep_ref, 2 * xl + c),
-        (recv_ref, 2 * (1 - xl) + c),
-        (keep2_ref, 2 * xl + 1 - c),
-        (recv2_ref, 2 * (1 - xl) + 1 - c),
-    ):
+    copies = [
+        pltpu.make_async_copy(ref, buf.at[n], sem.at[n])
+        for n, ref in enumerate((keep_ref, recv_ref, keep2_ref, recv2_ref))
+    ]
+    for copy in copies:
+        copy.start()
+    for n, row in enumerate((2 * xl + c, 2 * (1 - xl) + c, 2 * xl + 1 - c, 2 * (1 - xl) + 1 - c)):
+        copies[n].wait()
         at = pl.multiple_of(row * 32, 32)
         for b in range(9):
-            hi, lo = halves(ref[b])
+            hi, lo = halves(buf[n, b])
             hl[pl.ds(at, 32), 384 * b : 384 * b + 384] = hi
             hl[pl.ds(pl.multiple_of(128 + at, 32), 32), 384 * b : 384 * b + 384] = lo
     out_ref[...] = self_product(hl[...])
@@ -416,12 +418,22 @@
     return g[:, :128] + cross + jnp.transpose(cross)
 
 
-def edge_kernel(ids_ref, table_ref, got_ref, got2_ref, areas, inner_ref, out_ref, z, near, sel, full):
+def edge_kernel(
+    ids_ref, table_ref, got_hbm, got2_hbm, areas_hbm, inner_hbm, mine_ref, other_ref,
+    z, near, sel, full, got_ref, got2_ref, areas, sem,
+):
+    copies = [
+        pltpu.make_async_copy(src, dst, sem.at[n])
+        for n, (src, dst) in enumerate(((got_hbm, got_ref), (got2_hbm, got2_ref), (areas_hbm, areas), (inner_hbm, full)))
+    ]
+    for copy in copies:
+        copy.start()
     xl, c = lax.axis_index("xl"), lax.axis_index("c")
     chip = space_index() * 2 + xl
     first, last = chip == 0, chip == SAMP - 1
     lane = lanes_of((8, 128))
-    full[...] = inner_ref[...]
+    for copy in copies:
+        copy.wait()
 
     @pl.when(chip < SAMP)
     def _():
@@ -501,10 +513,8 @@
         hi, lo = halves((both[:128] + both[128:]) * jnp.concatenate(weight, axis=1))
         full[...] += self_product(jnp.concatenate([hi, lo], axis=0))
 
-    for k in range(2):
-        block = full[pl.ds(pl.multiple_of(64 * k + 32 * c, 32), 32), :]
-        out_ref[k] = block
-        out_ref[2 + k] = block
+    mine_ref[...] = full[pl.ds(pl.multiple_of(64 * xl + 32 * c, 32), 32), :]
+    other_ref[...] = full[pl.ds(pl.multiple_of(64 * (1 - xl) + 32 * c, 32), 32), :]
 
 
 def body(pw_field, cell_area, tile_ids, edge_table):
@@ -557,26 +567,35 @@
         inner_kernel,
         in_specs=[vm] * 4,
         out_specs=vm,
-        scratch_shapes=[pltpu.VMEM((256, 3456), BF16)],
+        scratch_shapes=[
+            pltpu.VMEM((4, 9, 32, 384), F32),
+            pltpu.VMEM((256, 3456), BF16),
+            pltpu.SemaphoreType.DMA((4,)),
+        ],
         out_shape=jax.ShapeDtypeStruct((128, 128), F32),
-        compiler_params=pltpu.CompilerParams(vmem_limit_bytes=VMEM_LIMIT),
+        compiler_params=pltpu.CompilerParams(vmem_limit_bytes=12 * 2**20),
         name="inner",
     )(keep, recv, keep2, recv2)
-    rows = pl.pallas_call(
+    mine, other = pl.pallas_call(
         edge_kernel,
         in_specs=[vm] * 6,
-        out_specs=vm,
+        out_specs=[vm] * 2,
         scratch_shapes=[
             pltpu.VMEM((1024, 128), F32),
             pltpu.VMEM((16, 128), jnp.int32),
             pltpu.VMEM((1024, 512), BF16),
             pltpu.VMEM((128, 128), F32),
+            pltpu.VMEM((512, 128), F32),
+            pltpu.VMEM((512, 128), F32),
+            pltpu.VMEM((64, 128), F32),
+            pltpu.SemaphoreType.DMA((4,)),
         ],
-        out_shape=jax.ShapeDtypeStruct((4, 32, 128), F32),
-        compiler_params=pltpu.CompilerParams(vmem_limit_bytes=VMEM_LIMIT),
+        out_shape=[jax.ShapeDtypeStruct((32, 128), F32)] * 2,
+        compiler_params=pltpu.CompilerParams(vmem_limit_bytes=12 * 2**20),
         name="edge",
     )(tile_ids.reshape(1, 96), table, got, got2, areas, inner)
-    line = jnp.sum(lax.all_to_all(rows, ("xh", "xl"), 0, 0), axis=0)
+    across = lax.ppermute(other, ("xh", "xl"), [(0, 3), (1, 2), (2, 1), (3, 0)])
+    line = mine + lax.ppermute(mine, "xh", flip) + lax.ppermute(other, "xl", flip) + across
     spread = jnp.broadcast_to(line[None], (16, 32, 128))
     return jnp.sum(lax.all_to_all(spread, ("y", "z"), 0, 0), axis=0) / (96 * SAMP * SAMP)
 

time: 67.4 us -> 61.3 us (0.909)
  blocking collectives: 20.3 us -> 11.4 us
  starting transfers between devices: 13.3 us -> 17.5 us
  Pallas kernels: 20.3 us -> 17.8 us
  waiting for transfers between devices: 10 us -> 12.5 us
  local copies, waits for them, and re-layouts: 2.28 us -> 1.04 us
    all_to_all x1 -> x0, blocking collectives: 8.87 us -> none  [body(): line = jnp.sum(lax.all_to_all(rows, ('xh', 'xl'), 0, 0), axis=0)]
    ppermute x0 -> x3, starting transfers between devices: none -> 4.17 us  [the longest x1 2.5 us: body(): across = lax.ppermute(other, ('xh', 'xl'), [(0, 3), (1, 2), (2, 1), (3, 0)])]
    ppermute x0 -> x3, waiting for transfers between devices: none -> 2.45 us  [the longest x1 1.3 us: body(): across = lax.ppermute(other, ('xh', 'xl'), [(0, 3), (1, 2), (2, 1), (3, 0)])]
    pallas_call x1, Pallas kernels: 3.76 us -> 2.29 us  [body(): pl.pallas_call(edge_kernel, in_specs=[vm] * 6, out_specs=[vm] * 2, scratc...]
    unnamed x10 -> x8, local copies, waits for them, and re-layouts: 2.26 us -> 1.02 us
    pallas_call x1, Pallas kernels: 3.05 us -> 2.03 us  [body(): pl.pallas_call(inner_kernel, in_specs=[vm] * 4, out_specs=vm, scratch_sha...]
  transfers between devices with their start and end apart: 5 -> 8, of which waited for: 1 -> 3; matrix products, arithmetic and copies ran while one was open for 0% -> 0% of each run, Pallas kernels for 5% -> 3%
where the time goes in v3:
time: 61.3 us; the launch traced here: 61 us
  Pallas kernels  17.8 us (29%)
  starting transfers between devices  17.5 us (29%)
  waiting for transfers between devices  12.5 us (20%)
  blocking collectives  11.4 us (19%)
  local copies, waits for them, and re-layouts  1.04 us (2%)
  other arithmetic  0.64 us (1%)
    pallas_call x1, Pallas kernels, body(): pl.pallas_call(filter_kernel, in_specs=[sm, sm] + [hbm] * 4 + [vm] * 3, o...  13.5 us
    all_to_all x1, blocking collectives, body(): lax.all_to_all(spread, ('y', 'z'), 0, 0)  11.4 us
    all_to_all x1, starting transfers between devices, body(): lax.all_to_all(edges.reshape(64, 8, 128), AXES[:4], 0, 0).reshape(512, 128)  11.1 us
    all_to_all x1, waiting for transfers between devices, body(): lax.all_to_all(edges.reshape(64, 8, 128), AXES[:4], 0, 0).reshape(512, 128)  10 us
    ppermute x1, starting transfers between devices, body(): across = lax.ppermute(other, ('xh', 'xl'), [(0, 3), (1, 2), (2, 1), (3, 0)])  2.5 us
    pallas_call x1, Pallas kernels, body(): pl.pallas_call(edge_kernel, in_specs=[vm] * 6, out_specs=[vm] * 2, scratc...  2.29 us
    pallas_call x1, Pallas kernels, body(): pl.pallas_call(inner_kernel, in_specs=[vm] * 4, out_specs=vm, scratch_sha...  2.03 us
    ppermute x1, starting transfers between devices, body(): recv = lax.ppermute(send, 'xl', flip)  1.65 us
  transfers between devices with their start and end apart: 8, of which 3 were waited for; matrix products, arithmetic and copies ran while one was open for 0% of the time, Pallas kernels for 3%

profile of v3, /device:TPU:0, one launch (start us, length us, event | category | flops | bytes accessed | tf_op | source)
XLA Modules:
  0.0 61.0 jit_solution(5264816509742828236)
XLA Ops:
  0.0 13.5 %filter.1 = (f32[9,32,384]{2,1,0:T(8,128)}, f32[9,32,384]{2,1,0:T(8,128)}, f32[512,128]{1,0:T(8,128)}, f32[64,128]{1,0:T(8,128)}) custom-call(s32[96]{0:T(128)} %ids.1, s32[3,4,96]{2,1,0:T(4,128)} %bitcast.6, f32[3,32,36864]{2,1,0:T(8,128)} %x_hbm.1, f32[16,36864]{1,0:T(8,128)} %area_hbm.1, bf16[2,1536,256]{2,1,0:T(8,128)(2,1)} %constant.16.clone.quad_hbm, ...), custom_call_target="tpu_custom_call" | custom-call | tf_op jit(solution)/shard_map/filter/pallas_call | solution.py:526
  13.5 0.0 copy-start.1
  13.5 0.0 copy-start.2
  13.5 0.0 copy-start.3
  13.5 1.7 %collective-permute-start.1 = (f32[9,32,384]{2,1,0:T(8,128)}, f32[9,32,384]{2,1,0:T(8,128)S(1)}, u32[]{:S(2)}, u32[]{:S(2)}) collective-permute-start(f32[9,32,384]{2,1,0:T(8,128)} %get-tuple-element.14), channel_id=1, source_target_pairs={{0,2},{2,0},{1,3},{3,1},{4,6},{6,4},{5,7},{7,5},{8,10},{10,8},{9,1... | collective-permute-start | bytes 1327112 | tf_op jit(solution)/shard_map/ppermute | solution.py:561
  15.2 11.1 %all-to-all-start = ((f32[64,8,128]{2,1,0:T(8,128)}), f32[64,8,128]{2,1,0:T(8,128)S(1)}, u32[]{:S(2)}, u32[]{:S(2)}) async-start(f32[64,8,128]{2,1,0:T(8,128)} %bitcast.9), calls=%async_computation | async-start | bytes 524288 | tf_op jit(solution)/shard_map/all_to_all | solution.py:563
  26.3 0.1 collective-permute-start.2
  26.4 0.0 collective-permute-done.1.recv_ref
  26.4 0.5 collective-permute-start.3
  26.9 10.0 %all-to-all-done = f32[64,8,128]{2,1,0:T(8,128)S(1)} async-done(((f32[64,8,128]{2,1,0:T(8,128)}), f32[64,8,128]{2,1,0:T(8,128)S(1)}, u32[]{:S(2)}, u32[]{:S(2)}) %all-to-all-start) | async-done | bytes 262176 | tf_op jit(solution)/shard_map/all_to_all | solution.py:563
  36.9 0.0 collective-permute-start
  36.9 0.0 collective-permute-done.2.keep2_ref
  36.9 0.0 collective-permute-done.3.recv2_ref
  36.9 0.0 copy-start
  36.9 1.0 %copy-done = f32[9,32,384]{2,1,0:T(8,128)S(1)} copy-done((f32[9,32,384]{2,1,0:T(8,128)S(1)}, f32[9,32,384]{2,1,0:T(8,128)}, u32[]{:S(2)}) %copy-start) | copy-done | bytes 442392
  37.9 2.0 %inner.1.inner_hbm = f32[128,128]{1,0:T(8,128)S(1)} custom-call(f32[9,32,384]{2,1,0:T(8,128)S(1)} %copy-done, f32[9,32,384]{2,1,0:T(8,128)S(1)} %collective-permute-done.1.recv_ref, f32[9,32,384]{2,1,0:T(8,128)S(1)} %collective-permute-done.2.keep2_ref, f32[9,32,384]{2,1,0:T(8,128)S(1)} %collective-permute-done.3.recv2_ref), custom_call_target="tpu_custom_call" | custom-call | tf_op jit(solution)/shard_map/inner/pallas_call | solution.py:566
  40.0 0.0 collective-permute-done.got2_hbm
  40.0 0.0 copy-done.1
  40.0 0.0 copy-done.2
  40.0 0.0 copy-done.3
  40.0 2.3 %edge.1 = (f32[32,128]{1,0:T(8,128)S(1)}, f32[32,128]{1,0:T(8,128)S(1)}) custom-call(s32[1,96]{1,0:T(1,128)S(1)} %bitcast.8, s32[3,4,96]{2,1,0:T(4,128)S(1)} %bitcast.7, f32[512,128]{1,0:T(8,128)S(1)} %bitcast.5, f32[512,128]{1,0:T(8,128)S(1)} %collective-permute-done.got2_hbm, f32[64,128]{1,0:T(8,128)S(1)} %copy-done.1, f32[128,128]{1,0:T(8,128)S(1)} %inner.1.inner_hbm), custom_call_target="tpu_custom_call" | custom-call | tf_op jit(solution)/shard_map/edge/pallas_call | solution.py:579
  42.3 1.0 %collective-permute-start.4 = (f32[32,128]{1,0:T(8,128)S(1)}, f32[32,128]{1,0:T(8,128)S(1)}, u32[]{:S(2)}, u32[]{:S(2)}) collective-permute-start(f32[32,128]{1,0:T(8,128)S(1)} %get-tuple-element.15), channel_id=1, source_target_pairs={{0,4},{4,0},{1,5},{5,1},{2,6},{6,2},{3,7},{7,3},{8,12},{12,8},{9,1... | collective-permute-start | bytes 49160 | tf_op jit(solution)/shard_map/ppermute | solution.py:598
  43.3 0.6 %collective-permute-start.5 = (f32[32,128]{1,0:T(8,128)S(1)}, f32[32,128]{1,0:T(8,128)S(1)}, u32[]{:S(2)}, u32[]{:S(2)}) collective-permute-start(f32[32,128]{1,0:T(8,128)S(1)} %get-tuple-element.16), channel_id=1, source_target_pairs={{0,2},{2,0},{1,3},{3,1},{4,6},{6,4},{5,7},{7,5},{8,10},{10,8},{9,1... | collective-permute-start | bytes 49160 | tf_op jit(solution)/shard_map/ppermute | solution.py:598
  44.0 2.5 %collective-permute-start.6 = (f32[32,128]{1,0:T(8,128)S(1)}, f32[32,128]{1,0:T(8,128)S(1)}, u32[]{:S(2)}, u32[]{:S(2)}) collective-permute-start(f32[32,128]{1,0:T(8,128)S(1)} %get-tuple-element.16), channel_id=1, source_target_pairs={{0,6},{2,4},{4,2},{6,0},{1,7},{3,5},{5,3},{7,1},{8,14},{10,12},{12... | collective-permute-start | bytes 49160 | tf_op jit(solution)/shard_map/ppermute | solution.py:597
  46.5 1.1 %collective-permute-done.4 = f32[32,128]{1,0:T(8,128)S(1)} collective-permute-done((f32[32,128]{1,0:T(8,128)S(1)}, f32[32,128]{1,0:T(8,128)S(1)}, u32[]{:S(2)}, u32[]{:S(2)}) %collective-permute-start.4) | collective-permute-done | bytes 16416 | tf_op jit(solution)/shard_map/ppermute | solution.py:598
  47.6 0.0 collective-permute-done.5
  47.6 1.3 %collective-permute-done.6 = f32[32,128]{1,0:T(8,128)S(1)} collective-permute-done((f32[32,128]{1,0:T(8,128)S(1)}, f32[32,128]{1,0:T(8,128)S(1)}, u32[]{:S(2)}, u32[]{:S(2)}) %collective-permute-start.6) | collective-permute-done | bytes 16416 | tf_op jit(solution)/shard_map/ppermute | solution.py:597
  49.0 11.4 %all_to_all.10 = f32[16,32,128]{2,1,0:T(8,128)S(1)} all-to-all(f32[16,32,128]{2,1,0:T(8,128)S(1)} %broadcast_in_dim.2), channel_id=1, replica_groups=mesh['y'=4,'z'=4,'xh'=2,'xl'=2,'c'=2] {'y','z'}, dimensions={0} | all-to-all | bytes 524288 | tf_op jit(solution)/shard_map/all_to_all | solution.py:600
  60.4 0.6 broadcast_multiply_fusion
  (3 shorter events, 0.1 us)
Async XLA Ops:
  13.5 26.5 %copy-start.1 = (f32[64,128]{1,0:T(8,128)S(1)}, f32[64,128]{1,0:T(8,128)}, u32[]{:S(2)}) copy-start(f32[64,128]{1,0:T(8,128)} %get-tuple-element.12.areas_hbm) | copy-start | bytes 98308
  13.5 26.5 %copy-start.2 = (s32[3,96,4]{1,2,0:T(4,128)S(1)}, s32[3,96,4]{1,2,0:T(4,128)}, u32[]{:S(2)}) copy-start(s32[3,96,4]{1,2,0:T(4,128)} %param.12) | copy-start | bytes 13828
  13.5 26.5 %copy-start.3 = (s32[96]{0:T(128)S(1)}, s32[96]{0:T(128)}, u32[]{:S(2)}) copy-start(s32[96]{0:T(128)} %ids.1) | copy-start | bytes 1156
  13.5 12.9 %collective-permute-start.1 = (f32[9,32,384]{2,1,0:T(8,128)}, f32[9,32,384]{2,1,0:T(8,128)S(1)}, u32[]{:S(2)}, u32[]{:S(2)}) collective-permute-start(f32[9,32,384]{2,1,0:T(8,128)} %get-tuple-element.14), channel_id=1, source_target_pairs={{0,2},{2,0},{1,3},{3,1},{4,6},{6,4},{5,7},{7,5},{8,10},{10,8},{9,1... | collective-permute-start | bytes 1327112 | tf_op jit(solution)/shard_map/ppermute | solution.py:561
  15.2 21.7 %all-to-all-start = ((f32[64,8,128]{2,1,0:T(8,128)}), f32[64,8,128]{2,1,0:T(8,128)S(1)}, u32[]{:S(2)}, u32[]{:S(2)}) async-start(f32[64,8,128]{2,1,0:T(8,128)} %bitcast.9), calls=%async_computation | async-start | bytes 524288 | tf_op jit(solution)/shard_map/all_to_all | solution.py:563
  26.3 10.6 %collective-permute-start.2 = (f32[9,32,384]{2,1,0:T(8,128)}, f32[9,32,384]{2,1,0:T(8,128)S(1)}, u32[]{:S(2)}, u32[]{:S(2)}) collective-permute-start(f32[9,32,384]{2,1,0:T(8,128)} %get-tuple-element.13.keep_ref), channel_id=1, source_target_pairs={{0,1},{1,0},{2,3},{3,2},{4,5},{5,4},{6,7},{7,6},{8,9},{9,8},{10,11... | collective-permute-start | bytes 1327112 | tf_op jit(solution)/shard_map/ppermute | solution.py:562
  26.4 10.5 %collective-permute-start.3 = (f32[9,32,384]{2,1,0:T(8,128)S(1)}, f32[9,32,384]{2,1,0:T(8,128)S(1)}, u32[]{:S(2)}, u32[]{:S(2)}) collective-permute-start(f32[9,32,384]{2,1,0:T(8,128)S(1)} %collective-permute-done.1.recv_ref), channel_id=1, source_target_pairs={{0,1},{1,0},{2,3},{3,2},{4,5},{5,4},{6,7},{7,6},{8,9},{9,8},{10,11... | collective-permute-start | bytes 1327112 | tf_op jit(solution)/shard_map/ppermute | solution.py:565
  36.9 3.1 %collective-permute-start = (f32[512,128]{1,0:T(8,128)S(1)}, f32[512,128]{1,0:T(8,128)S(1)}, u32[]{:S(2)}, u32[]{:S(2)}) collective-permute-start(f32[512,128]{1,0:T(8,128)S(1)} %bitcast.4), channel_id=1, source_target_pairs={{0,1},{1,0},{2,3},{3,2},{4,5},{5,4},{6,7},{7,6},{8,9},{9,8},{10,11... | collective-permute-start | bytes 786440 | tf_op jit(solution)/shard_map/ppermute | solution.py:564
  36.9 1.0 %copy-start = (f32[9,32,384]{2,1,0:T(8,128)S(1)}, f32[9,32,384]{2,1,0:T(8,128)}, u32[]{:S(2)}) copy-start(f32[9,32,384]{2,1,0:T(8,128)} %get-tuple-element.13.keep_ref) | copy-start | bytes 1327108
  42.3 5.3 %collective-permute-start.4 = (f32[32,128]{1,0:T(8,128)S(1)}, f32[32,128]{1,0:T(8,128)S(1)}, u32[]{:S(2)}, u32[]{:S(2)}) collective-permute-start(f32[32,128]{1,0:T(8,128)S(1)} %get-tuple-element.15), channel_id=1, source_target_pairs={{0,4},{4,0},{1,5},{5,1},{2,6},{6,2},{3,7},{7,3},{8,12},{12,8},{9,1... | collective-permute-start | bytes 49160 | tf_op jit(solution)/shard_map/ppermute | solution.py:598
  43.3 4.3 %collective-permute-start.5 = (f32[32,128]{1,0:T(8,128)S(1)}, f32[32,128]{1,0:T(8,128)S(1)}, u32[]{:S(2)}, u32[]{:S(2)}) collective-permute-start(f32[32,128]{1,0:T(8,128)S(1)} %get-tuple-element.16), channel_id=1, source_target_pairs={{0,2},{2,0},{1,3},{3,1},{4,6},{6,4},{5,7},{7,5},{8,10},{10,8},{9,1... | collective-permute-start | bytes 49160 | tf_op jit(solution)/shard_map/ppermute | solution.py:598
  44.0 4.9 %collective-permute-start.6 = (f32[32,128]{1,0:T(8,128)S(1)}, f32[32,128]{1,0:T(8,128)S(1)}, u32[]{:S(2)}, u32[]{:S(2)}) collective-permute-start(f32[32,128]{1,0:T(8,128)S(1)} %get-tuple-element.16), channel_id=1, source_target_pairs={{0,6},{2,4},{4,2},{6,0},{1,7},{3,5},{5,3},{7,1},{8,14},{10,12},{12... | collective-permute-start | bytes 49160 | tf_op jit(solution)/shard_map/ppermute | solution.py:597

commit v4 on v3

--- a/solution.py
+++ b/solution.py
@@ -178,9 +178,10 @@
 
 
 def filter_kernel(
-    ids, table, x_hbm, area_hbm, quad_hbm, colm_hbm, rowm_ref, small_ref, mask_ref,
+    ids_hbm, table_hbm, x_hbm, area_hbm, quad_hbm, colm_hbm, rowm_hbm, small_hbm, mask_hbm,
     keep_ref, send_ref, edge_ref, areas_ref,
-    xs, area, quads, colm, wp, lhs, stage, root, packed, lrow, lcol, strip, sem_x, sem_a, sem_c,
+    xs, area, quads, colm, wp, lhs, stage, root, packed, lrow, lcol, strip, ids, table, rowm_ref, small_ref, mask_ref,
+    sem_x, sem_a, sem_c,
 ):
     xl = lax.axis_index("xl")
     lane = lanes_of((SB, 128))
@@ -196,14 +197,28 @@
 
     copy_quads = pltpu.make_async_copy(quad_hbm, quads, sem_c.at[0])
     copy_colm = pltpu.make_async_copy(colm_hbm, colm, sem_c.at[1])
+    early = [
+        pltpu.make_async_copy(src, dst, sem_c.at[2 + n])
+        for n, (src, dst) in enumerate(((ids_hbm, ids), (table_hbm, table), (small_hbm, small_ref)))
+    ]
+    late = [
+        pltpu.make_async_copy(src, dst, sem_c.at[5 + n])
+        for n, (src, dst) in enumerate(((rowm_hbm, rowm_ref), (mask_hbm, mask_ref)))
+    ]
+    for copy in early:
+        copy.start()
     for part in range(2):
         copy_area(part).start()
         copy_x(0, part).start()
+    for copy in late:
+        copy.start()
     wp[:, :PAD] = jnp.zeros((SB, PAD), F32)
     wp[:, PAD + CELLS :] = jnp.zeros((SB, 512), F32)
     strip[:, 96:, :] = jnp.zeros((8, 32, 128), F32)
     stage[...] = jnp.zeros((2, 2, 16, 1536), F32)
     wide = lambda k: jnp.concatenate([k, k], axis=1)
+    for copy in early + late:
+        copy.wait()
     near = [wide(small_ref[d : d + 1, :]) for d in range(5)]
     far = [wide(small_ref[5 + d : 6 + d, :]) for d in range(2)]
     lane2 = lanes_of((SB, 256))
@@ -525,7 +540,7 @@
     hbm = pl.BlockSpec(memory_space=pl.ANY)
     keep, send, edges, areas = pl.pallas_call(
         filter_kernel,
-        in_specs=[sm, sm] + [hbm] * 4 + [vm] * 3,
+        in_specs=[hbm] * 9,
         out_specs=[vm] * 4,
         scratch_shapes=[
             pltpu.VMEM((3, SB, CELLS), F32),
@@ -540,9 +555,14 @@
             pltpu.VMEM((384, 256), BF16),
             pltpu.VMEM((192, 1536), BF16),
             pltpu.VMEM((8, 128, 128), F32),
+            pltpu.SMEM((96,), jnp.int32),
+            pltpu.SMEM((3, 4, 96), jnp.int32),
+            pltpu.VMEM((256, 128), BF16),
+            pltpu.VMEM((32, 128), F32),
+            pltpu.VMEM((8, 384), F32),
             pltpu.SemaphoreType.DMA((3 * PARTS,)),
             pltpu.SemaphoreType.DMA((PARTS,)),
-            pltpu.SemaphoreType.DMA((2,)),
+            pltpu.SemaphoreType.DMA((7,)),
         ],
         out_shape=[
             jax.ShapeDtypeStruct((9, 32, 384), F32),

time: 61.3 us -> 60.8 us (level)
  no operation moved by 1% of the time
where the time goes in v4:
time: 60.8 us; the launch traced here: 60.5 us
  starting transfers between devices  17.5 us (29%)
  Pallas kernels  17.3 us (28%)
  waiting for transfers between devices  12.5 us (21%)
  blocking collectives  11.4 us (19%)
  local copies, waits for them, and re-layouts  1.04 us (2%)
  other arithmetic  0.64 us (1%)
    pallas_call x1, Pallas kernels, body(): pl.pallas_call(filter_kernel, in_specs=[hbm] * 9, out_specs=[vm] * 4, scr...  13 us
    all_to_all x1, blocking collectives, body(): lax.all_to_all(spread, ('y', 'z'), 0, 0)  11.4 us
    all_to_all x1, starting transfers between devices, body(): lax.all_to_all(edges.reshape(64, 8, 128), AXES[:4], 0, 0).reshape(512, 128)  11.1 us
    all_to_all x1, waiting for transfers between devices, body(): lax.all_to_all(edges.reshape(64, 8, 128), AXES[:4], 0, 0).reshape(512, 128)  10 us
    ppermute x1, starting transfers between devices, body(): across = lax.ppermute(other, ('xh', 'xl'), [(0, 3), (1, 2), (2, 1), (3, 0)])  2.5 us
    pallas_call x1, Pallas kernels, body(): pl.pallas_call(edge_kernel, in_specs=[vm] * 6, out_specs=[vm] * 2, scratc...  2.29 us
    pallas_call x1, Pallas kernels, body(): pl.pallas_call(inner_kernel, in_specs=[vm] * 4, out_specs=vm, scratch_sha...  2.03 us
    ppermute x1, starting transfers between devices, body(): recv = lax.ppermute(send, 'xl', flip)  1.65 us
  transfers between devices with their start and end apart: 8, of which 3 were waited for; matrix products, arithmetic and copies ran while one was open for 0% of the time, Pallas kernels for 3%

profile of v4, /device:TPU:0, one launch (start us, length us, event | category | flops | bytes accessed | tf_op | source)
XLA Modules:
  0.0 60.5 jit_solution(6427686819414850647)
XLA Ops:
  0.0 13.0 %filter.1 = (f32[9,32,384]{2,1,0:T(8,128)}, f32[9,32,384]{2,1,0:T(8,128)}, f32[512,128]{1,0:T(8,128)}, f32[64,128]{1,0:T(8,128)}) custom-call(s32[96]{0:T(128)} %ids_hbm.1, s32[3,4,96]{2,1,0:T(4,128)} %bitcast.6, f32[3,32,36864]{2,1,0:T(8,128)} %x_hbm.1, f32[16,36864]{1,0:T(8,128)} %area_hbm.1, bf16[2,1536,256]{2,1,0:T(8,128)(2,1)} %constant.16.clone.quad_hbm, ...), custom_call_target="tpu_custom_call" | custom-call | tf_op jit(solution)/shard_map/filter/pallas_call | solution.py:541
  13.0 0.0 copy-start.1
  13.0 0.0 copy-start.2
  13.0 0.0 copy-start.3
  13.0 1.6 %collective-permute-start.1 = (f32[9,32,384]{2,1,0:T(8,128)}, f32[9,32,384]{2,1,0:T(8,128)S(1)}, u32[]{:S(2)}, u32[]{:S(2)}) collective-permute-start(f32[9,32,384]{2,1,0:T(8,128)} %get-tuple-element.14), channel_id=1, source_target_pairs={{0,2},{2,0},{1,3},{3,1},{4,6},{6,4},{5,7},{7,5},{8,10},{10,8},{9,1... | collective-permute-start | bytes 1327112 | tf_op jit(solution)/shard_map/ppermute | solution.py:581
  14.7 11.1 %all-to-all-start = ((f32[64,8,128]{2,1,0:T(8,128)}), f32[64,8,128]{2,1,0:T(8,128)S(1)}, u32[]{:S(2)}, u32[]{:S(2)}) async-start(f32[64,8,128]{2,1,0:T(8,128)} %bitcast.9), calls=%async_computation | async-start | bytes 524288 | tf_op jit(solution)/shard_map/all_to_all | solution.py:583
  25.8 0.1 collective-permute-start.2
  25.9 0.0 collective-permute-done.1.recv_ref
  25.9 0.5 collective-permute-start.3
  26.4 10.0 %all-to-all-done = f32[64,8,128]{2,1,0:T(8,128)S(1)} async-done(((f32[64,8,128]{2,1,0:T(8,128)}), f32[64,8,128]{2,1,0:T(8,128)S(1)}, u32[]{:S(2)}, u32[]{:S(2)}) %all-to-all-start) | async-done | bytes 262176 | tf_op jit(solution)/shard_map/all_to_all | solution.py:583
  36.4 0.0 collective-permute-start
  36.4 0.0 collective-permute-done.2.keep2_ref
  36.4 0.0 collective-permute-done.3.recv2_ref
  36.4 0.0 copy-start
  36.4 1.0 %copy-done = f32[9,32,384]{2,1,0:T(8,128)S(1)} copy-done((f32[9,32,384]{2,1,0:T(8,128)S(1)}, f32[9,32,384]{2,1,0:T(8,128)}, u32[]{:S(2)}) %copy-start) | copy-done | bytes 442392
  37.4 2.0 %inner.1.inner_hbm = f32[128,128]{1,0:T(8,128)S(1)} custom-call(f32[9,32,384]{2,1,0:T(8,128)S(1)} %copy-done, f32[9,32,384]{2,1,0:T(8,128)S(1)} %collective-permute-done.1.recv_ref, f32[9,32,384]{2,1,0:T(8,128)S(1)} %collective-permute-done.2.keep2_ref, f32[9,32,384]{2,1,0:T(8,128)S(1)} %collective-permute-done.3.recv2_ref), custom_call_target="tpu_custom_call" | custom-call | tf_op jit(solution)/shard_map/inner/pallas_call | solution.py:586
  39.5 0.0 collective-permute-done.got2_hbm
  39.5 0.0 copy-done.1
  39.5 0.0 copy-done.2
  39.5 0.0 copy-done.3
  39.5 2.3 %edge.1 = (f32[32,128]{1,0:T(8,128)S(1)}, f32[32,128]{1,0:T(8,128)S(1)}) custom-call(s32[1,96]{1,0:T(1,128)S(1)} %bitcast.8, s32[3,4,96]{2,1,0:T(4,128)S(1)} %bitcast.7, f32[512,128]{1,0:T(8,128)S(1)} %bitcast.5, f32[512,128]{1,0:T(8,128)S(1)} %collective-permute-done.got2_hbm, f32[64,128]{1,0:T(8,128)S(1)} %copy-done.1, f32[128,128]{1,0:T(8,128)S(1)} %inner.1.inner_hbm), custom_call_target="tpu_custom_call" | custom-call | tf_op jit(solution)/shard_map/edge/pallas_call | solution.py:599
  41.8 1.0 %collective-permute-start.4 = (f32[32,128]{1,0:T(8,128)S(1)}, f32[32,128]{1,0:T(8,128)S(1)}, u32[]{:S(2)}, u32[]{:S(2)}) collective-permute-start(f32[32,128]{1,0:T(8,128)S(1)} %get-tuple-element.15), channel_id=1, source_target_pairs={{0,4},{4,0},{1,5},{5,1},{2,6},{6,2},{3,7},{7,3},{8,12},{12,8},{9,1... | collective-permute-start | bytes 49160 | tf_op jit(solution)/shard_map/ppermute | solution.py:618
  42.8 0.6 %collective-permute-start.5 = (f32[32,128]{1,0:T(8,128)S(1)}, f32[32,128]{1,0:T(8,128)S(1)}, u32[]{:S(2)}, u32[]{:S(2)}) collective-permute-start(f32[32,128]{1,0:T(8,128)S(1)} %get-tuple-element.16), channel_id=1, source_target_pairs={{0,2},{2,0},{1,3},{3,1},{4,6},{6,4},{5,7},{7,5},{8,10},{10,8},{9,1... | collective-permute-start | bytes 49160 | tf_op jit(solution)/shard_map/ppermute | solution.py:618
  43.5 2.5 %collective-permute-start.6 = (f32[32,128]{1,0:T(8,128)S(1)}, f32[32,128]{1,0:T(8,128)S(1)}, u32[]{:S(2)}, u32[]{:S(2)}) collective-permute-start(f32[32,128]{1,0:T(8,128)S(1)} %get-tuple-element.16), channel_id=1, source_target_pairs={{0,6},{2,4},{4,2},{6,0},{1,7},{3,5},{5,3},{7,1},{8,14},{10,12},{12... | collective-permute-start | bytes 49160 | tf_op jit(solution)/shard_map/ppermute | solution.py:617
  46.0 1.1 %collective-permute-done.4 = f32[32,128]{1,0:T(8,128)S(1)} collective-permute-done((f32[32,128]{1,0:T(8,128)S(1)}, f32[32,128]{1,0:T(8,128)S(1)}, u32[]{:S(2)}, u32[]{:S(2)}) %collective-permute-start.4) | collective-permute-done | bytes 16416 | tf_op jit(solution)/shard_map/ppermute | solution.py:618
  47.1 0.0 collective-permute-done.5
  47.1 1.3 %collective-permute-done.6 = f32[32,128]{1,0:T(8,128)S(1)} collective-permute-done((f32[32,128]{1,0:T(8,128)S(1)}, f32[32,128]{1,0:T(8,128)S(1)}, u32[]{:S(2)}, u32[]{:S(2)}) %collective-permute-start.6) | collective-permute-done | bytes 16416 | tf_op jit(solution)/shard_map/ppermute | solution.py:617
  48.5 11.4 %all_to_all.10 = f32[16,32,128]{2,1,0:T(8,128)S(1)} all-to-all(f32[16,32,128]{2,1,0:T(8,128)S(1)} %broadcast_in_dim.2), channel_id=1, replica_groups=mesh['y'=4,'z'=4,'xh'=2,'xl'=2,'c'=2] {'y','z'}, dimensions={0} | all-to-all | bytes 524288 | tf_op jit(solution)/shard_map/all_to_all | solution.py:620
  59.9 0.6 %broadcast_multiply_fusion = f32[32,128]{1,0:T(8,128)} fusion(f32[32,128]{1,0:T(8,128)S(1)} %reduce_sum.9), kind=kLoop, calls=%fused_computation.1 | loop fusion | flops 4096 | bytes 32768 | tf_op jit(solution)/shard_map/div | solution.py:620
  (3 shorter events, 0.0 us)
Async XLA Ops:
  13.0 26.5 %copy-start.1 = (f32[64,128]{1,0:T(8,128)S(1)}, f32[64,128]{1,0:T(8,128)}, u32[]{:S(2)}) copy-start(f32[64,128]{1,0:T(8,128)} %get-tuple-element.12.areas_hbm) | copy-start | bytes 98308
  13.0 26.5 %copy-start.2 = (s32[3,96,4]{1,2,0:T(4,128)S(1)}, s32[3,96,4]{1,2,0:T(4,128)}, u32[]{:S(2)}) copy-start(s32[3,96,4]{1,2,0:T(4,128)} %param.12) | copy-start | bytes 13828
  13.0 26.5 %copy-start.3 = (s32[96]{0:T(128)S(1)}, s32[96]{0:T(128)}, u32[]{:S(2)}) copy-start(s32[96]{0:T(128)} %ids_hbm.1) | copy-start | bytes 1156
  13.0 12.9 %collective-permute-start.1 = (f32[9,32,384]{2,1,0:T(8,128)}, f32[9,32,384]{2,1,0:T(8,128)S(1)}, u32[]{:S(2)}, u32[]{:S(2)}) collective-permute-start(f32[9,32,384]{2,1,0:T(8,128)} %get-tuple-element.14), channel_id=1, source_target_pairs={{0,2},{2,0},{1,3},{3,1},{4,6},{6,4},{5,7},{7,5},{8,10},{10,8},{9,1... | collective-permute-start | bytes 1327112 | tf_op jit(solution)/shard_map/ppermute | solution.py:581
  14.7 21.7 %all-to-all-start = ((f32[64,8,128]{2,1,0:T(8,128)}), f32[64,8,128]{2,1,0:T(8,128)S(1)}, u32[]{:S(2)}, u32[]{:S(2)}) async-start(f32[64,8,128]{2,1,0:T(8,128)} %bitcast.9), calls=%async_computation | async-start | bytes 524288 | tf_op jit(solution)/shard_map/all_to_all | solution.py:583
  25.8 10.6 %collective-permute-start.2 = (f32[9,32,384]{2,1,0:T(8,128)}, f32[9,32,384]{2,1,0:T(8,128)S(1)}, u32[]{:S(2)}, u32[]{:S(2)}) collective-permute-start(f32[9,32,384]{2,1,0:T(8,128)} %get-tuple-element.13.keep_ref), channel_id=1, source_target_pairs={{0,1},{1,0},{2,3},{3,2},{4,5},{5,4},{6,7},{7,6},{8,9},{9,8},{10,11... | collective-permute-start | bytes 1327112 | tf_op jit(solution)/shard_map/ppermute | solution.py:582
  25.9 10.5 %collective-permute-start.3 = (f32[9,32,384]{2,1,0:T(8,128)S(1)}, f32[9,32,384]{2,1,0:T(8,128)S(1)}, u32[]{:S(2)}, u32[]{:S(2)}) collective-permute-start(f32[9,32,384]{2,1,0:T(8,128)S(1)} %collective-permute-done.1.recv_ref), channel_id=1, source_target_pairs={{0,1},{1,0},{2,3},{3,2},{4,5},{5,4},{6,7},{7,6},{8,9},{9,8},{10,11... | collective-permute-start | bytes 1327112 | tf_op jit(solution)/shard_map/ppermute | solution.py:585
  36.4 3.1 %collective-permute-start = (f32[512,128]{1,0:T(8,128)S(1)}, f32[512,128]{1,0:T(8,128)S(1)}, u32[]{:S(2)}, u32[]{:S(2)}) collective-permute-start(f32[512,128]{1,0:T(8,128)S(1)} %bitcast.4), channel_id=1, source_target_pairs={{0,1},{1,0},{2,3},{3,2},{4,5},{5,4},{6,7},{7,6},{8,9},{9,8},{10,11... | collective-permute-start | bytes 786440 | tf_op jit(solution)/shard_map/ppermute | solution.py:584
  36.4 1.0 %copy-start = (f32[9,32,384]{2,1,0:T(8,128)S(1)}, f32[9,32,384]{2,1,0:T(8,128)}, u32[]{:S(2)}) copy-start(f32[9,32,384]{2,1,0:T(8,128)} %get-tuple-element.13.keep_ref) | copy-start | bytes 1327108
  41.8 5.3 %collective-permute-start.4 = (f32[32,128]{1,0:T(8,128)S(1)}, f32[32,128]{1,0:T(8,128)S(1)}, u32[]{:S(2)}, u32[]{:S(2)}) collective-permute-start(f32[32,128]{1,0:T(8,128)S(1)} %get-tuple-element.15), channel_id=1, source_target_pairs={{0,4},{4,0},{1,5},{5,1},{2,6},{6,2},{3,7},{7,3},{8,12},{12,8},{9,1... | collective-permute-start | bytes 49160 | tf_op jit(solution)/shard_map/ppermute | solution.py:618
  42.8 4.3 %collective-permute-start.5 = (f32[32,128]{1,0:T(8,128)S(1)}, f32[32,128]{1,0:T(8,128)S(1)}, u32[]{:S(2)}, u32[]{:S(2)}) collective-permute-start(f32[32,128]{1,0:T(8,128)S(1)} %get-tuple-element.16), channel_id=1, source_target_pairs={{0,2},{2,0},{1,3},{3,1},{4,6},{6,4},{5,7},{7,5},{8,10},{10,8},{9,1... | collective-permute-start | bytes 49160 | tf_op jit(solution)/shard_map/ppermute | solution.py:618
  43.5 4.9 %collective-permute-start.6 = (f32[32,128]{1,0:T(8,128)S(1)}, f32[32,128]{1,0:T(8,128)S(1)}, u32[]{:S(2)}, u32[]{:S(2)}) collective-permute-start(f32[32,128]{1,0:T(8,128)S(1)} %get-tuple-element.16), channel_id=1, source_target_pairs={{0,6},{2,4},{4,2},{6,0},{1,7},{3,5},{5,3},{7,1},{8,14},{10,12},{12... | collective-permute-start | bytes 49160 | tf_op jit(solution)/shard_map/ppermute | solution.py:617

commit v5 on v4

--- a/solution.py
+++ b/solution.py
@@ -181,7 +181,7 @@
     ids_hbm, table_hbm, x_hbm, area_hbm, quad_hbm, colm_hbm, rowm_hbm, small_hbm, mask_hbm,
     keep_ref, send_ref, edge_ref, areas_ref,
     xs, area, quads, colm, wp, lhs, stage, root, packed, lrow, lcol, strip, ids, table, rowm_ref, small_ref, mask_ref,
-    sem_x, sem_a, sem_c,
+    sem_x, sem_a, sem_c, sem_o,
 ):
     xl = lax.axis_index("xl")
     lane = lanes_of((SB, 128))
@@ -228,6 +228,13 @@
     def win(off):
         return wp[:, PAD + off : PAD + off + 256]
 
+    def give(tile):
+        to = pl.ds(3 * tile, 3)
+        return [
+            pltpu.make_async_copy(packed.at[tile, pl.ds(3 * side, 3)], ref.at[to], sem_o.at[2 * tile + n])
+            for n, (side, ref) in enumerate(((xl, keep_ref), (1 - xl, send_ref)))
+        ]
+
     def collect(tile):
         if tile == 0:
             copy_quads.wait()
@@ -255,17 +262,17 @@
         for g in range(6):
             a, b = out_a[SB * g : SB * g + SB], out_b[SB * g : SB * g + SB]
             a1, b0 = a[:, 128:], b[:, :128]
-            packed[g, :, 0:128] = a[:, :128] * root[g : g + 1, 0:128]
-            packed[g, :, 128:256] = jnp.where(lane < 64, a1, b0) * root[g : g + 1, 128:256]
-            packed[g, :, 256:384] = b[:, 128:] * root[g : g + 1, 256:384]
+            packed[tile, g, :, 0:128] = a[:, :128] * root[g : g + 1, 0:128]
+            packed[tile, g, :, 128:256] = jnp.where(lane < 64, a1, b0) * root[g : g + 1, 128:256]
+            packed[tile, g, :, 256:384] = b[:, 128:] * root[g : g + 1, 256:384]
             at_a = (lane >= 8 * g) & (lane < 8 * g + 4)
             at_b = (lane >= 8 * g + 4) & (lane < 8 * g + 8)
             left = jnp.where(at_a, pltpu.roll(a1, (8 * g + 64) % 128, 1), left)
             left = jnp.where(at_b, pltpu.roll(b0, (8 * g + 4) % 128, 1), left)
             right = jnp.where(at_a, pltpu.roll(a1, (8 * g + 60) % 128, 1), right)
             right = jnp.where(at_b, b0 if g == 0 else pltpu.roll(b0, 8 * g, 1), right)
-        keep_ref[3 * tile : 3 * tile + 3] = packed[pl.ds(3 * xl, 3)]
-        send_ref[3 * tile : 3 * tile + 3] = packed[pl.ds(3 * (1 - xl), 3)]
+        for copy in give(tile):
+            copy.start()
         here = slice(32 * tile, 32 * tile + 32)
         strip[4, here, :] = out_a[:SB, :128]
         strip[5, here, :] = swap_ends(pltpu.roll(out_b[160:192, 128:], 48, 1), lane)
@@ -407,6 +414,9 @@
         if e >= 2:
             v = jnp.where(ends, 0.0, v)
         areas_ref[16 * e : 16 * e + 16, :] = v
+    for tile in range(3):
+        for copy in give(tile):
+            copy.wait()
 
 
 def inner_kernel(keep_ref, recv_ref, keep2_ref, recv2_ref, out_ref, buf, hl, sem):
@@ -541,7 +551,7 @@
     keep, send, edges, areas = pl.pallas_call(
         filter_kernel,
         in_specs=[hbm] * 9,
-        out_specs=[vm] * 4,
+        out_specs=[hbm, hbm, vm, vm],
         scratch_shapes=[
             pltpu.VMEM((3, SB, CELLS), F32),
             pltpu.VMEM((16, CELLS), F32),
@@ -551,7 +561,7 @@
             pltpu.VMEM((2, 2, 432, 1536), BF16),
             pltpu.VMEM((2, 2, 16, 1536), F32),
             pltpu.VMEM((8, 384), F32),
-            pltpu.VMEM((6, SB, 384), F32),
+            pltpu.VMEM((3, 6, SB, 384), F32),
             pltpu.VMEM((384, 256), BF16),
             pltpu.VMEM((192, 1536), BF16),
             pltpu.VMEM((8, 128, 128), F32),
@@ -563,6 +573,7 @@
             pltpu.SemaphoreType.DMA((3 * PARTS,)),
             pltpu.SemaphoreType.DMA((PARTS,)),
             pltpu.SemaphoreType.DMA((7,)),
+            pltpu.SemaphoreType.DMA((6,)),
         ],
         out_shape=[
             jax.ShapeDtypeStruct((9, 32, 384), F32),

time: 60.8 us -> 60.8 us (level)
  no operation moved by 1% of the time
where the time goes in v5:
time: 60.8 us; the launch traced here: 60.5 us
  starting transfers between devices  17.5 us (29%)
  Pallas kernels  17.3 us (28%)
  waiting for transfers between devices  12.5 us (21%)
  blocking collectives  11.4 us (19%)
  local copies, waits for them, and re-layouts  1.04 us (2%)
  other arithmetic  0.64 us (1%)
    pallas_call x1, Pallas kernels, body(): pl.pallas_call(filter_kernel, in_specs=[hbm] * 9, out_specs=[hbm, hbm, vm...  13 us
    all_to_all x1, blocking collectives, body(): lax.all_to_all(spread, ('y', 'z'), 0, 0)  11.4 us
    all_to_all x1, starting transfers between devices, body(): lax.all_to_all(edges.reshape(64, 8, 128), AXES[:4], 0, 0).reshape(512, 128)  11.1 us
    all_to_all x1, waiting for transfers between devices, body(): lax.all_to_all(edges.reshape(64, 8, 128), AXES[:4], 0, 0).reshape(512, 128)  10 us
    ppermute x1, starting transfers between devices, body(): across = lax.ppermute(other, ('xh', 'xl'), [(0, 3), (1, 2), (2, 1), (3, 0)])  2.5 us
    pallas_call x1, Pallas kernels, body(): pl.pallas_call(edge_kernel, in_specs=[vm] * 6, out_specs=[vm] * 2, scratc...  2.29 us
    pallas_call x1, Pallas kernels, body(): pl.pallas_call(inner_kernel, in_specs=[vm] * 4, out_specs=vm, scratch_sha...  2.04 us
    ppermute x1, starting transfers between devices, body(): recv = lax.ppermute(send, 'xl', flip)  1.66 us
  transfers between devices with their start and end apart: 8, of which 3 were waited for; matrix products, arithmetic and copies ran while one was open for 0% of the time, Pallas kernels for 3%

profile of v5, /device:TPU:0, one launch (start us, length us, event | category | flops | bytes accessed | tf_op | source)
XLA Modules:
  0.0 60.5 jit_solution(10429112802037176129)
XLA Ops:
  0.0 13.0 %filter.1 = (f32[9,32,384]{2,1,0:T(8,128)}, f32[9,32,384]{2,1,0:T(8,128)}, f32[512,128]{1,0:T(8,128)}, f32[64,128]{1,0:T(8,128)}) custom-call(s32[96]{0:T(128)} %ids_hbm.1, s32[3,4,96]{2,1,0:T(4,128)} %bitcast.6, f32[3,32,36864]{2,1,0:T(8,128)} %x_hbm.1, f32[16,36864]{1,0:T(8,128)} %area_hbm.1, bf16[2,1536,256]{2,1,0:T(8,128)(2,1)} %constant.16.clone.quad_hbm, ...), custom_call_target="tpu_custom_call" | custom-call | tf_op jit(solution)/shard_map/filter/pallas_call | solution.py:551
  13.0 0.0 copy-start.1
  13.0 0.0 copy-start.2
  13.0 0.0 copy-start.3
  13.0 1.7 %collective-permute-start.1 = (f32[9,32,384]{2,1,0:T(8,128)}, f32[9,32,384]{2,1,0:T(8,128)S(1)}, u32[]{:S(2)}, u32[]{:S(2)}) collective-permute-start(f32[9,32,384]{2,1,0:T(8,128)} %get-tuple-element.14), channel_id=1, source_target_pairs={{0,2},{2,0},{1,3},{3,1},{4,6},{6,4},{5,7},{7,5},{8,10},{10,8},{9,1... | collective-permute-start | bytes 1327112 | tf_op jit(solution)/shard_map/ppermute | solution.py:592
  14.7 11.1 %all-to-all-start = ((f32[64,8,128]{2,1,0:T(8,128)}), f32[64,8,128]{2,1,0:T(8,128)S(1)}, u32[]{:S(2)}, u32[]{:S(2)}) async-start(f32[64,8,128]{2,1,0:T(8,128)} %bitcast.9), calls=%async_computation | async-start | bytes 524288 | tf_op jit(solution)/shard_map/all_to_all | solution.py:594
  25.8 0.1 collective-permute-start.2
  25.9 0.0 collective-permute-done.1.recv_ref
  25.9 0.5 collective-permute-start.3
  26.4 10.0 %all-to-all-done = f32[64,8,128]{2,1,0:T(8,128)S(1)} async-done(((f32[64,8,128]{2,1,0:T(8,128)}), f32[64,8,128]{2,1,0:T(8,128)S(1)}, u32[]{:S(2)}, u32[]{:S(2)}) %all-to-all-start) | async-done | bytes 262176 | tf_op jit(solution)/shard_map/all_to_all | solution.py:594
  36.4 0.0 collective-permute-start
  36.4 0.0 collective-permute-done.2.keep2_ref
  36.4 0.0 collective-permute-done.3.recv2_ref
  36.4 0.0 copy-start
  36.4 1.0 %copy-done = f32[9,32,384]{2,1,0:T(8,128)S(1)} copy-done((f32[9,32,384]{2,1,0:T(8,128)S(1)}, f32[9,32,384]{2,1,0:T(8,128)}, u32[]{:S(2)}) %copy-start) | copy-done | bytes 442392
  37.4 2.0 %inner.1.inner_hbm = f32[128,128]{1,0:T(8,128)S(1)} custom-call(f32[9,32,384]{2,1,0:T(8,128)S(1)} %copy-done, f32[9,32,384]{2,1,0:T(8,128)S(1)} %collective-permute-done.1.recv_ref, f32[9,32,384]{2,1,0:T(8,128)S(1)} %collective-permute-done.2.keep2_ref, f32[9,32,384]{2,1,0:T(8,128)S(1)} %collective-permute-done.3.recv2_ref), custom_call_target="tpu_custom_call" | custom-call | tf_op jit(solution)/shard_map/inner/pallas_call | solution.py:597
  39.5 0.0 collective-permute-done.got2_hbm
  39.5 0.0 copy-done.1
  39.5 0.0 copy-done.2
  39.5 0.0 copy-done.3
  39.5 2.3 %edge.1 = (f32[32,128]{1,0:T(8,128)S(1)}, f32[32,128]{1,0:T(8,128)S(1)}) custom-call(s32[1,96]{1,0:T(1,128)S(1)} %bitcast.8, s32[3,4,96]{2,1,0:T(4,128)S(1)} %bitcast.7, f32[512,128]{1,0:T(8,128)S(1)} %bitcast.5, f32[512,128]{1,0:T(8,128)S(1)} %collective-permute-done.got2_hbm, f32[64,128]{1,0:T(8,128)S(1)} %copy-done.1, f32[128,128]{1,0:T(8,128)S(1)} %inner.1.inner_hbm), custom_call_target="tpu_custom_call" | custom-call | tf_op jit(solution)/shard_map/edge/pallas_call | solution.py:610
  41.8 1.0 %collective-permute-start.4 = (f32[32,128]{1,0:T(8,128)S(1)}, f32[32,128]{1,0:T(8,128)S(1)}, u32[]{:S(2)}, u32[]{:S(2)}) collective-permute-start(f32[32,128]{1,0:T(8,128)S(1)} %get-tuple-element.15), channel_id=1, source_target_pairs={{0,4},{4,0},{1,5},{5,1},{2,6},{6,2},{3,7},{7,3},{8,12},{12,8},{9,1... | collective-permute-start | bytes 49160 | tf_op jit(solution)/shard_map/ppermute | solution.py:629
  42.9 0.6 %collective-permute-start.5 = (f32[32,128]{1,0:T(8,128)S(1)}, f32[32,128]{1,0:T(8,128)S(1)}, u32[]{:S(2)}, u32[]{:S(2)}) collective-permute-start(f32[32,128]{1,0:T(8,128)S(1)} %get-tuple-element.16), channel_id=1, source_target_pairs={{0,2},{2,0},{1,3},{3,1},{4,6},{6,4},{5,7},{7,5},{8,10},{10,8},{9,1... | collective-permute-start | bytes 49160 | tf_op jit(solution)/shard_map/ppermute | solution.py:629
  43.5 2.5 %collective-permute-start.6 = (f32[32,128]{1,0:T(8,128)S(1)}, f32[32,128]{1,0:T(8,128)S(1)}, u32[]{:S(2)}, u32[]{:S(2)}) collective-permute-start(f32[32,128]{1,0:T(8,128)S(1)} %get-tuple-element.16), channel_id=1, source_target_pairs={{0,6},{2,4},{4,2},{6,0},{1,7},{3,5},{5,3},{7,1},{8,14},{10,12},{12... | collective-permute-start | bytes 49160 | tf_op jit(solution)/shard_map/ppermute | solution.py:628
  46.0 1.1 %collective-permute-done.4 = f32[32,128]{1,0:T(8,128)S(1)} collective-permute-done((f32[32,128]{1,0:T(8,128)S(1)}, f32[32,128]{1,0:T(8,128)S(1)}, u32[]{:S(2)}, u32[]{:S(2)}) %collective-permute-start.4) | collective-permute-done | bytes 16416 | tf_op jit(solution)/shard_map/ppermute | solution.py:629
  47.2 0.0 collective-permute-done.5
  47.2 1.3 %collective-permute-done.6 = f32[32,128]{1,0:T(8,128)S(1)} collective-permute-done((f32[32,128]{1,0:T(8,128)S(1)}, f32[32,128]{1,0:T(8,128)S(1)}, u32[]{:S(2)}, u32[]{:S(2)}) %collective-permute-start.6) | collective-permute-done | bytes 16416 | tf_op jit(solution)/shard_map/ppermute | solution.py:628
  48.5 11.4 %all_to_all.10 = f32[16,32,128]{2,1,0:T(8,128)S(1)} all-to-all(f32[16,32,128]{2,1,0:T(8,128)S(1)} %broadcast_in_dim.2), channel_id=1, replica_groups=mesh['y'=4,'z'=4,'xh'=2,'xl'=2,'c'=2] {'y','z'}, dimensions={0} | all-to-all | bytes 524288 | tf_op jit(solution)/shard_map/all_to_all | solution.py:631
  59.9 0.6 %broadcast_multiply_fusion = f32[32,128]{1,0:T(8,128)} fusion(f32[32,128]{1,0:T(8,128)S(1)} %reduce_sum.9), kind=kLoop, calls=%fused_computation.1 | loop fusion | flops 4096 | bytes 32768 | tf_op jit(solution)/shard_map/div | solution.py:631
  (3 shorter events, 0.1 us)
Async XLA Ops:
  13.0 26.5 %copy-start.1 = (f32[64,128]{1,0:T(8,128)S(1)}, f32[64,128]{1,0:T(8,128)}, u32[]{:S(2)}) copy-start(f32[64,128]{1,0:T(8,128)} %get-tuple-element.12.areas_hbm) | copy-start | bytes 98308
  13.0 26.5 %copy-start.2 = (s32[3,96,4]{1,2,0:T(4,128)S(1)}, s32[3,96,4]{1,2,0:T(4,128)}, u32[]{:S(2)}) copy-start(s32[3,96,4]{1,2,0:T(4,128)} %param.12) | copy-start | bytes 13828
  13.0 26.5 %copy-start.3 = (s32[96]{0:T(128)S(1)}, s32[96]{0:T(128)}, u32[]{:S(2)}) copy-start(s32[96]{0:T(128)} %ids_hbm.1) | copy-start | bytes 1156
  13.0 12.9 %collective-permute-start.1 = (f32[9,32,384]{2,1,0:T(8,128)}, f32[9,32,384]{2,1,0:T(8,128)S(1)}, u32[]{:S(2)}, u32[]{:S(2)}) collective-permute-start(f32[9,32,384]{2,1,0:T(8,128)} %get-tuple-element.14), channel_id=1, source_target_pairs={{0,2},{2,0},{1,3},{3,1},{4,6},{6,4},{5,7},{7,5},{8,10},{10,8},{9,1... | collective-permute-start | bytes 1327112 | tf_op jit(solution)/shard_map/ppermute | solution.py:592
  14.7 21.7 %all-to-all-start = ((f32[64,8,128]{2,1,0:T(8,128)}), f32[64,8,128]{2,1,0:T(8,128)S(1)}, u32[]{:S(2)}, u32[]{:S(2)}) async-start(f32[64,8,128]{2,1,0:T(8,128)} %bitcast.9), calls=%async_computation | async-start | bytes 524288 | tf_op jit(solution)/shard_map/all_to_all | solution.py:594
  25.8 10.6 %collective-permute-start.2 = (f32[9,32,384]{2,1,0:T(8,128)}, f32[9,32,384]{2,1,0:T(8,128)S(1)}, u32[]{:S(2)}, u32[]{:S(2)}) collective-permute-start(f32[9,32,384]{2,1,0:T(8,128)} %get-tuple-element.13.keep_ref), channel_id=1, source_target_pairs={{0,1},{1,0},{2,3},{3,2},{4,5},{5,4},{6,7},{7,6},{8,9},{9,8},{10,11... | collective-permute-start | bytes 1327112 | tf_op jit(solution)/shard_map/ppermute | solution.py:593
  25.9 10.5 %collective-permute-start.3 = (f32[9,32,384]{2,1,0:T(8,128)S(1)}, f32[9,32,384]{2,1,0:T(8,128)S(1)}, u32[]{:S(2)}, u32[]{:S(2)}) collective-permute-start(f32[9,32,384]{2,1,0:T(8,128)S(1)} %collective-permute-done.1.recv_ref), channel_id=1, source_target_pairs={{0,1},{1,0},{2,3},{3,2},{4,5},{5,4},{6,7},{7,6},{8,9},{9,8},{10,11... | collective-permute-start | bytes 1327112 | tf_op jit(solution)/shard_map/ppermute | solution.py:596
  36.4 3.1 %collective-permute-start = (f32[512,128]{1,0:T(8,128)S(1)}, f32[512,128]{1,0:T(8,128)S(1)}, u32[]{:S(2)}, u32[]{:S(2)}) collective-permute-start(f32[512,128]{1,0:T(8,128)S(1)} %bitcast.4), channel_id=1, source_target_pairs={{0,1},{1,0},{2,3},{3,2},{4,5},{5,4},{6,7},{7,6},{8,9},{9,8},{10,11... | collective-permute-start | bytes 786440 | tf_op jit(solution)/shard_map/ppermute | solution.py:595
  36.4 1.0 %copy-start = (f32[9,32,384]{2,1,0:T(8,128)S(1)}, f32[9,32,384]{2,1,0:T(8,128)}, u32[]{:S(2)}) copy-start(f32[9,32,384]{2,1,0:T(8,128)} %get-tuple-element.13.keep_ref) | copy-start | bytes 1327108
  41.8 5.3 %collective-permute-start.4 = (f32[32,128]{1,0:T(8,128)S(1)}, f32[32,128]{1,0:T(8,128)S(1)}, u32[]{:S(2)}, u32[]{:S(2)}) collective-permute-start(f32[32,128]{1,0:T(8,128)S(1)} %get-tuple-element.15), channel_id=1, source_target_pairs={{0,4},{4,0},{1,5},{5,1},{2,6},{6,2},{3,7},{7,3},{8,12},{12,8},{9,1... | collective-permute-start | bytes 49160 | tf_op jit(solution)/shard_map/ppermute | solution.py:629
  42.9 4.3 %collective-permute-start.5 = (f32[32,128]{1,0:T(8,128)S(1)}, f32[32,128]{1,0:T(8,128)S(1)}, u32[]{:S(2)}, u32[]{:S(2)}) collective-permute-start(f32[32,128]{1,0:T(8,128)S(1)} %get-tuple-element.16), channel_id=1, source_target_pairs={{0,2},{2,0},{1,3},{3,1},{4,6},{6,4},{5,7},{7,5},{8,10},{10,8},{9,1... | collective-permute-start | bytes 49160 | tf_op jit(solution)/shard_map/ppermute | solution.py:629
  43.5 4.9 %collective-permute-start.6 = (f32[32,128]{1,0:T(8,128)S(1)}, f32[32,128]{1,0:T(8,128)S(1)}, u32[]{:S(2)}, u32[]{:S(2)}) collective-permute-start(f32[32,128]{1,0:T(8,128)S(1)} %get-tuple-element.16), channel_id=1, source_target_pairs={{0,6},{2,4},{4,2},{6,0},{1,7},{3,5},{5,3},{7,1},{8,14},{10,12},{12... | collective-permute-start | bytes 49160 | tf_op jit(solution)/shard_map/ppermute | solution.py:628
